TPU v7x, 128 devices: a whole 4x4x4 slice. The times are simulated.
128 devices in a mesh: row: 16 (over x, z), col: 8 (over y, core).
Axes of the slice: x: 4, y: 4, z: 4, core: 2. Of those that a mesh axis runs over, the one named last changes fastest.
Arguments:
- x_tiles: float32 [16, 8, 12, 128, 128], P('row', 'col'), as said below
- block_rows: int32 [16, 8, 12], P('row', 'col'), may hold values from 0 to 48, as said below
- block_cols: int32 [16, 8, 12], P('row', 'col'), may hold values from 0 to 48, as said below
- pair_left: int32 [16, 8, 276], P('row', 'col'), may hold values from 0 to 95, as said below
- pair_right: int32 [16, 8, 276], P('row', 'col'), may hold values from 0 to 191, as said below
- pair_target: int32 [16, 8, 276], P('row', 'col'), may hold values from 0 to 12, as said below
- branches: int32 [4], replicated, may hold values from 0 to 1, as said below
Outputs:
- purified: float32 [16, 8, 12, 128, 128], P('row', 'col')
- traces: float32 [4, 2], replicated
Inputs may be any that keep to these rules, and one draw needn't show every extreme that they name: `x_tiles`: X is symmetric and zero outside its stored pattern; a slot that holds no block is zero. The stored pattern is symmetric and holds every diagonal block; every block-row stores the same number of blocks; the block-rows of a device are 3 labels that form its row strip, shared by the devices of that strip; a device stores each position once; a slot that holds no block has block_rows = block_cols = 48; some device uses all 12 slots. `block_cols`: the block-columns of a device are 6 labels that form its column strip, shared by the devices of that strip; 48 marks a slot that holds no block. `pair_left`: for each stored block (i, j) of a device, its list holds exactly one entry for every k with (i, k) and (k, j) both stored, and no other used entry. Unused entries hold 0. `pair_right`: unused entries hold 0. `pair_target`: used entries come first on each device; a target of 12 marks an unused entry; on some device all 276 entries are used. Both branches occur among the steps.
All inputs are finite; a program needn't handle non-finite values.
Results may differ from a plain program's by a relative error of at most 0.0003.
Values sent between devices are 32-bit elements; how exact they have to be, the bound alone decides.
A program may use at most 192 MiB of HBM per device.

v0:
```python
import jax
import jax.numpy as jnp
from jax import lax
from jax.sharding import PartitionSpec as P

BR = 3
STEPS = 4


def slot_products(strip_left, strip_right, left_ids, right_ids, target_ids, slot_count):
    left_blocks = jnp.take(strip_left, left_ids, axis=0)
    right_blocks = jnp.take(strip_right, right_ids, axis=0)
    block_product = jnp.einsum(
        "pij,pjk->pik", left_blocks, right_blocks, precision=lax.Precision.HIGHEST
    )
    weights = (target_ids[:, None] == jnp.arange(slot_count, dtype=jnp.int32)[None, :]).astype(
        jnp.float32
    )
    return jnp.einsum("ps,pik->sik", weights, block_product, precision=lax.Precision.HIGHEST)


def grouped_products(strip_left, strip_right, left_ids, right_ids, target_ids, slot_count):
    pair_count = left_ids.shape[0]
    group_size = pair_count * 4 // slot_count
    live_count = jnp.sum((target_ids < slot_count).astype(jnp.int32))
    rounds = (live_count + group_size - 1) // group_size
    empty = jnp.zeros((slot_count, strip_left.shape[1], strip_left.shape[2]), jnp.float32)

    def one_round(turn_index, running):
        first_pair = turn_index * group_size
        left_part = lax.dynamic_slice_in_dim(left_ids, first_pair, group_size)
        right_part = lax.dynamic_slice_in_dim(right_ids, first_pair, group_size)
        target_part = lax.dynamic_slice_in_dim(target_ids, first_pair, group_size)
        return running + slot_products(
            strip_left, strip_right, left_part, right_part, target_part, slot_count
        )

    return lax.fori_loop(0, rounds, one_round, empty)


def diagonal_sum(stored, is_diagonal):
    sums = jnp.sum(jnp.diagonal(stored, axis1=-2, axis2=-1), axis=-1)
    return jnp.sum(jnp.where(is_diagonal, sums, jnp.zeros_like(sums)))


def body(x_tiles, block_rows, block_cols, pair_left, pair_right, pair_target, branches):
    stored = x_tiles[0, 0]
    slot_count = stored.shape[0]
    block_order = stored.shape[-1]
    side_blocks = lax.axis_size("row") * BR
    is_diagonal = (block_rows[0, 0] == block_cols[0, 0]) & (block_rows[0, 0] < side_blocks)
    left_ids = pair_left[0, 0]
    right_ids = pair_right[0, 0]
    target_ids = pair_target[0, 0]
    scale = 1.0 / (side_blocks * block_order)
    step_terms = []
    for step_index in range(STEPS):
        strip_left = lax.all_gather(stored, "col", axis=0, tiled=True)
        strip_right = lax.all_gather(stored, "row", axis=0, tiled=True)
        squared = grouped_products(
            strip_left, strip_right, left_ids, right_ids, target_ids, slot_count
        )
        terms = jnp.stack([diagonal_sum(stored, is_diagonal), diagonal_sum(squared, is_diagonal)])
        step_terms.append(lax.psum(terms, ("row", "col")))
        stored = jnp.where(branches[step_index] == 1, squared, 2.0 * stored - squared)
    traces = jnp.stack(step_terms)
    return (stored[None, None], traces * scale)


def solution(mesh):
    placed = (
        P("row", "col", None, None, None),
        P("row", "col", None),
        P("row", "col", None),
        P("row", "col", None),
        P("row", "col", None),
        P("row", "col", None),
        P(),
    )
    return jax.shard_map(
        body,
        mesh=mesh,
        in_specs=placed,
        out_specs=(P("row", "col", None, None, None), P()),
        check_vma=False,
    )
```

profile of v0, /device:TPU:1, one launch (start us, length us, event | category | flops | bytes accessed | tf_op | source)
XLA Modules:
  0.0 1094.7 jit_solution(13326007199445795616)
XLA Ops:
  18.1 36.2 %all-gather.23.cloned.1.call-done = f32[1,1,96,128,128]{4,3,1,0,2:T(8,128)} async-done(((f32[1,1,12,128,128]{4,3,1,0,2:T(8,128)}), f32[1,1,96,128,128]{4,3,1,0,2:T(8,128)}) %all-gather.23.cloned.1.call-update) | async-done | bytes 6291472 | tf_op jit(solution)/shard_map/all_gather | solution.py:58
  54.3 92.0 %all-gather.25.cloned.1.call-done = f32[1,1,192,128,128]{4,3,1,0,2:T(8,128)} async-done(((f32[1,1,12,128,128]{4,3,1,0,2:T(8,128)}), f32[1,1,192,128,128]{4,3,1,0,2:T(8,128)}) %all-gather.25.cloned.1.call-update) | async-done | bytes 12582928 | tf_op jit(solution)/shard_map/all_gather | solution.py:59
  146.4 91.7 %while.40 = (s32[]{:T(128)}, f32[12,128,128]{2,0,1:T(8,128)S(1)}, s32[]{:T(128)}, s32[276]{0:T(512)S(1)}, s32[276]{0:T(512)S(1)}, /*index=5*/f32[96,128,128]{2,1...) while((s32[]{:T(128)}, f32[12,128,128]{2,0,1:T(8,128)S(1)}, ...), condition=%wide.region_2.0_spmd, body=%wide.region_1.4_spmd.sunk | while | flops 2535526400 | bytes 49820140 | solution.py:38
  160.9 10.2 fusion.98
  191.4 10.2 fusion.98
  221.9 10.2 fusion.98
  242.8 12.0 %subtract_select_fusion.3 = f32[12,128,128]{0,2,1:T(8,128)} fusion(f32[12,128,128]{0,2,1:T(8,128)} %copy.34, pred[]{:T(512)} %bitcast.7, f32[1,1,12,128,128]{2,4,3,1,0:T(8,128)} %copy.32), kind=kLoop, calls=%fused_computation.95 | loop fusion | flops 589824 | bytes 2359297 | tf_op jit(solution)/shard_map/jit(_where)/select_n | solution.py:65
  262.1 39.8 %all-gather.11.cloned.1.call-done = f32[96,128,128]{2,1,0:T(8,128)} async-done(((f32[12,128,128]{2,1,0:T(8,128)}), f32[96,128,128]{2,1,0:T(8,128)}) %all-gather.11.cloned.1.call-update) | async-done | bytes 6291472 | tf_op jit(solution)/shard_map/all_gather | solution.py:58
  301.9 92.4 %all-gather.13.cloned.1.call-done = f32[192,128,128]{2,1,0:T(8,128)} async-done(((f32[12,128,128]{2,1,0:T(8,128)}), f32[192,128,128]{2,1,0:T(8,128)}) %all-gather.13.cloned.1.call-update) | async-done | bytes 12582928 | tf_op jit(solution)/shard_map/all_gather | solution.py:59
  394.4 101.2 %while.41 = (s32[]{:T(128)}, f32[12,128,128]{2,0,1:T(8,128)S(1)}, s32[]{:T(128)}, s32[276]{0:T(512)S(1)}, s32[276]{0:T(512)S(1)}, /*index=5*/f32[96,128,128]{2,1...) while((s32[]{:T(128)}, f32[12,128,128]{2,0,1:T(8,128)S(1)}, ...), condition=%wide.region_4.7_spmd, body=%wide.region_3.6_spmd.sunk | while | flops 2535526400 | bytes 49820140 | solution.py:38
  408.9 10.2 fusion.104
  439.4 10.2 fusion.104
  469.9 10.2 fusion.104
  500.2 12.0 %subtract_select_fusion.2 = f32[12,128,128]{0,2,1:T(8,128)} fusion(f32[12,128,128]{0,2,1:T(8,128)} %copy.38, f32[12,128,128]{0,2,1:T(8,128)} %subtract_select_fusion.3, pred[]{:T(512)} %bitcast.6), kind=kLoop, calls=%fused_computation.94 | loop fusion | flops 589824 | bytes 2359297 | tf_op jit(solution)/shard_map/jit(_where)/select_n | solution.py:65
  519.4 39.8 %all-gather.15.cloned.1.call-done = f32[96,128,128]{2,1,0:T(8,128)} async-done(((f32[12,128,128]{2,1,0:T(8,128)}), f32[96,128,128]{2,1,0:T(8,128)}) %all-gather.15.cloned.1.call-update) | async-done | bytes 6291472 | tf_op jit(solution)/shard_map/all_gather | solution.py:58
  559.3 92.4 %all-gather.17.cloned.1.call-done = f32[192,128,128]{2,1,0:T(8,128)} async-done(((f32[12,128,128]{2,1,0:T(8,128)}), f32[192,128,128]{2,1,0:T(8,128)}) %all-gather.17.cloned.1.call-update) | async-done | bytes 12582928 | tf_op jit(solution)/shard_map/all_gather | solution.py:59
  651.8 91.7 %while.42 = (s32[]{:T(128)}, f32[12,128,128]{2,0,1:T(8,128)S(1)}, s32[]{:T(128)}, s32[276]{0:T(512)S(1)}, s32[276]{0:T(512)S(1)}, /*index=5*/f32[96,128,128]{2,1...) while((s32[]{:T(128)}, f32[12,128,128]{2,0,1:T(8,128)S(1)}, ...), condition=%wide.region_6.9_spmd, body=%wide.region_5.8_spmd.sunk | while | flops 2535526400 | bytes 49820140 | solution.py:38
  696.8 10.2 fusion.110
  748.2 12.0 %subtract_select_fusion.1 = f32[12,128,128]{0,2,1:T(8,128)} fusion(f32[12,128,128]{0,2,1:T(8,128)} %copy.42, f32[12,128,128]{0,2,1:T(8,128)} %subtract_select_fusion.2, pred[]{:T(512)} %bitcast.5), kind=kLoop, calls=%fused_computation.93 | loop fusion | flops 589824 | bytes 2359297 | tf_op jit(solution)/shard_map/jit(_where)/select_n | solution.py:65
  780.6 26.7 %all-gather.19.cloned.1.call-done = f32[96,128,128]{2,1,0:T(8,128)} async-done(((f32[12,128,128]{2,1,0:T(8,128)}), f32[96,128,128]{2,1,0:T(8,128)}) %all-gather.19.cloned.1.call-update) | async-done | bytes 6291472 | tf_op jit(solution)/shard_map/all_gather | solution.py:58
  807.3 92.6 %all-gather.21.cloned.1.call-done = f32[192,128,128]{2,1,0:T(8,128)} async-done(((f32[12,128,128]{2,1,0:T(8,128)}), f32[192,128,128]{2,1,0:T(8,128)}) %all-gather.21.cloned.1.call-update) | async-done | bytes 12582928 | tf_op jit(solution)/shard_map/all_gather | solution.py:59
  900.0 92.0 %while.43 = (s32[]{:T(128)}, f32[12,128,128]{2,0,1:T(8,128)S(1)}, s32[]{:T(128)}, s32[276]{0:T(512)S(1)}, s32[276]{0:T(512)S(1)}, /*index=5*/f32[96,128,128]{2,1...) while((s32[]{:T(128)}, f32[12,128,128]{2,0,1:T(8,128)S(1)}, ...), condition=%wide.region_8.11_spmd, body=%wide.region_7.10_spmd.sunk | while | flops 2535526400 | bytes 49820140 | solution.py:38
  998.4 11.9 %fusion.60 = f32[1,1,12,128,128]{2,4,3,1,0:T(8,128)} fusion(f32[12,128,128]{0,2,1:T(8,128)} %copy.46, f32[12,128,128]{0,2,1:T(8,128)} %subtract_select_fusion.1, pred[]{:T(512)} %bitcast.4), kind=kLoop, calls=%fused_computation.96 | loop fusion | flops 589824 | bytes 2359297 | tf_op jit(solution)/shard_map/broadcast_in_dim | solution.py:67
  1022.2 64.5 %all-reduce = (f32[1,2]{1,0:T(1,128)S(1)}, f32[1,2]{1,0:T(1,128)S(1)}, f32[1,2]{1,0:T(1,128)S(1)}, f32[1,2]{1,0:T(1,128)S(1)}) all-reduce(f32[1,2]{1,0:T(1,128)S(1)} %get-tuple-element.315, f32[1,2]{1,0:T(1,128)S(1)} %get-tuple-element.314, f32[1,2]{1,0:T(1,128)S(1)} %get-tuple-element.313, ...), channel_id=1, replica_groups=mesh['row'=16,'col'=8] {'row','col'}, use_global_device_ids=true, to_apply=%region_28.31 | all-reduce | flops 8 | bytes 64 | tf_op jit(solution)/shard_map/psum | solution.py:64
  (155 shorter events, 369.7 us)
Async XLA Ops:
  7.2 9.5 copy-start.1
  7.2 9.6 copy-start.2
  7.2 9.6 copy-start
  7.2 47.1 %all-gather.23.cloned.1.call-start = ((), (), s32[]{:S(2)}) async-start(), calls=%async_computation.6 | async-start | bytes 7077888 | tf_op jit(solution)/shard_map/all_gather | solution.py:58
  7.9 138.4 %all-gather.25.cloned.1.call-start = ((), (), s32[]{:S(2)}) async-start(), calls=%async_computation.7 | async-start | bytes 13369344 | tf_op jit(solution)/shard_map/all_gather | solution.py:59
  8.7 293.2 %all-gather.11.cloned.1.call-start = ((), (), s32[]{:S(2)}) async-start(), calls=%async_computation | async-start | bytes 7077888 | tf_op jit(solution)/shard_map/all_gather | solution.py:58
  260.8 133.5 %all-gather.13.cloned.1.call-start = ((), (), s32[]{:S(2)}) async-start(), calls=%async_computation.1 | async-start | bytes 13369344 | tf_op jit(solution)/shard_map/all_gather | solution.py:59
  261.4 297.9 %all-gather.15.cloned.1.call-start = ((), (), s32[]{:S(2)}) async-start(), calls=%async_computation.2 | async-start | bytes 7077888 | tf_op jit(solution)/shard_map/all_gather | solution.py:58
  518.2 133.5 %all-gather.17.cloned.1.call-start = ((), (), s32[]{:S(2)}) async-start(), calls=%async_computation.3 | async-start | bytes 13369344 | tf_op jit(solution)/shard_map/all_gather | solution.py:59
  518.8 288.6 %all-gather.19.cloned.1.call-start = ((), (), s32[]{:S(2)}) async-start(), calls=%async_computation.4 | async-start | bytes 7077888 | tf_op jit(solution)/shard_map/all_gather | solution.py:58
  766.2 133.7 %all-gather.21.cloned.1.call-start = ((), (), s32[]{:S(2)}) async-start(), calls=%async_computation.5 | async-start | bytes 13369344 | tf_op jit(solution)/shard_map/all_gather | solution.py:59
  1010.3 6.1 copy-start.3
  1010.3 6.1 copy-start.4
Sparse Core Ops, SparseCore 0:
  9.7 44.5 all-gather.22
  56.5 89.7 all-gather.24
  260.9 40.9 all-gather.10
  304.5 89.7 all-gather.12
  518.3 40.9 all-gather.14
  561.9 89.7 all-gather.16
  766.4 40.9 all-gather.18
  810.1 89.7 all-gather.20
where the time goes:
time: 1100 us; the launch traced here: 1090 us
  waiting for transfers between devices  515 us (47%)
  local copies, waits for them, and re-layouts  237 us (22%)
  matrix products  191 us (17%)
  blocking collectives  64.5 us (6%)
  other arithmetic  56.4 us (5%)
  between operations  17.9 us (2%)
  loops' own time  11.4 us (1%)
    all_gather x4, waiting for transfers between devices, body(): strip_right = lax.all_gather(stored, 'row', axis=0, tiled=True)  369 us
    all_gather x4, waiting for transfers between devices, body(): strip_left = lax.all_gather(stored, 'col', axis=0, tiled=True)  143 us
    dot_general x12, matrix products, slot_products(): jnp.einsum('pij,pjk->pik', left_blocks, right_blocks, precision=lax.Preci...  122 us
    gather x12, local copies, waits for them, and re-layouts, slot_products(): right_blocks = jnp.take(strip_right, right_ids, axis=0)  96.4 us
    gather x12, local copies, waits for them, and re-layouts, slot_products(): left_blocks = jnp.take(strip_left, left_ids, axis=0)  75.4 us
    dot_general x12, matrix products, slot_products(): jnp.einsum('ps,pik->sik', weights, block_product, precision=lax.Precision...  69.3 us
    psum x1, blocking collectives, body(): step_terms.append(lax.psum(terms, ('row', 'col')))  64.5 us
    select_n x3, other arithmetic, body(): jnp.where(branches[step_index] == 1, squared, 2.0 * stored - squared)  36 us
  transfers between devices with their start and end apart: 8, of which 8 were waited for; matrix products, arithmetic and copies ran while one was open for 2% of the time, Pallas kernels for 0%

commit v1 on v0

v1 whole, which is shorter than its diff:
```python
import jax
import jax.numpy as jnp
from jax import lax
from jax.experimental import pallas as pl
from jax.experimental.pallas import tpu as pltpu
from jax.sharding import PartitionSpec as P

MESH = pl.DeviceIdType.MESH
BR = 3
STEPS = 4
BLK = 128
SLOTS = 12
ROWS = 16
COLS = 8
DEPTH = 32
CHUNKS = 4
CS = SLOTS // CHUNKS
GROUP = 8


def zbits(z):
    low = ((z + 1) // 2) % 2
    high = z // 2
    return low, high


def kernel(table, coef, x_hbm, out_hbm, tr, xs, lf, rf, ls, rs, acc, r_l, r_r, s_l, s_r, sw_s, sw_r, fin_s, fin_r, credit):
    row = lax.axis_index("row")
    col = lax.axis_index("col")
    x, z, y, p = row // 4, row % 4, col // 2, col % 2
    low, high = zbits(z)
    moved = p != low

    z_low = z + 1 - 2 * (z % 2)
    z_high = 3 - z
    partner = (x * 4 + z_low, y * 2 + 1 - p)
    sibling = (row, y * 2 + 1 - p)
    l_next = (row, ((y + 1) % 4) * 2 + p)
    l_prev = (row, ((y + 3) % 4) * 2 + p)
    l_pair = (x * 4 + z_low, col)
    r_next = (((x + 1) % 4) * 4 + z, col)
    r_prev = (((x + 3) % 4) * 4 + z, col)
    r_pair = (x * 4 + z_high, col)
    neighbours = (l_next, l_prev, l_pair, r_next, r_prev, r_pair, sibling)

    barrier = pltpu.get_barrier_semaphore()
    for device in neighbours + (partner,):
        pl.semaphore_signal(barrier, inc=1, device_id=device, device_id_type=MESH)
    pl.semaphore_wait(barrier, len(neighbours) + 1)

    def roles(q, h, unit):
        a, b, c = (q + 3) % 4, (q + 1) % 4, (q + 2) % 4
        g = 1 - h
        return [unit(q, h), unit(a, h), unit(b, h), unit(q, g), unit(c, h), unit(a, g), unit(b, g), unit(c, g)]

    units_l = roles(y, low, lambda q, h: q * 2 + h)
    units_r = roles(x, high, lambda q, h: q * 4 + h * 3 + p * (1 - 2 * h))
    units_s = roles(x, high, lambda q, h: q * 4 + h * 3 + (1 - p) * (1 - 2 * h))

    def part(m):
        return pl.ds(m * CS, CS)

    def copy(src, dst, ssem, rsem, device):
        return pltpu.make_async_remote_copy(
            src_ref=src, dst_ref=dst, send_sem=ssem, recv_sem=rsem, device_id=device, device_id_type=MESH
        )

    class Gather:
        def __init__(self, buf, units, rsem, ssem, nxt, prv, pair):
            self.buf, self.units, self.rsem, self.ssem = buf, units, rsem, ssem
            self.nxt, self.prv, self.pair = nxt, prv, pair

        def source(self, role, m):
            return xs.at[part(m)] if role == 0 else self.buf.at[self.units[role], part(m)]

        def plan(self, m):
            nxt, prv, pair = self.nxt, self.prv, self.pair
            first = [(0, nxt, 1), (0, prv, 2), (0, pair, 3)]
            second = [(1, nxt, 4)] if m % 2 == 0 else [(2, prv, 4)]
            if m < CHUNKS // 2:
                second += [(1, pair, 5), (2, pair, 6)]
                third = [(4, pair, 7)]
            else:
                second += [(3, nxt, 5), (3, prv, 6)]
                third = [(5, nxt, 7)] if m % 2 == 0 else [(6, prv, 7)]
            return first, second, third

        def sends(self, m, level):
            plan = self.plan(m)
            at = sum(len(one) for one in plan[:level])
            made = []
            for index, (role, device, there) in enumerate(plan[level]):
                made.append(
                    copy(
                        self.source(role, m),
                        self.buf.at[self.units[role], part(m)],
                        self.ssem.at[m, at + index],
                        self.rsem.at[m, there - 1],
                        device,
                    )
                )
            return made

        def arrived(self, m, role):
            place = self.buf.at[self.units[role], part(m)]
            copy(place, place, self.ssem.at[m, 0], self.rsem.at[m, role - 1], self.nxt).wait_recv()

    left = Gather(lf, units_l, r_l, s_l, l_next, l_prev, l_pair)
    right = Gather(rf, units_r, r_r, s_r, r_next, r_prev, r_pair)

    def share(m, role):
        place = rf.at[units_r[role], part(m)]
        return copy(right.source(role, m), place, s_r.at[m, 7 + role], r_r.at[m, 7 + role], sibling)

    def shared(m, role):
        place = rf.at[units_s[role], part(m)]
        copy(place, place, s_r.at[m, 0], r_r.at[m, 7 + role], sibling).wait_recv()

    def send_own(m):
        for one in left.sends(m, 0) + right.sends(m, 0) + [share(m, 0)]:
            one.start()

    def split(value):
        top = value.astype(jnp.bfloat16)
        return top, (value - top.astype(jnp.float32)).astype(jnp.bfloat16)

    def keep_left(unit, block, value):
        top, low_part = split(value)
        ls[unit * SLOTS + block, 0:BLK] = top
        ls[unit * SLOTS + block, BLK : 2 * BLK] = low_part

    def keep_right(unit, block, value):
        top, low_part = split(value)
        rs[unit * SLOTS + block, :, 0:BLK] = top
        rs[unit * SLOTS + block, :, BLK : 2 * BLK] = low_part

    def prepare_left(m, role):
        unit = units_l[role]

        @pl.loop(m * CS, (m + 1) * CS)
        def _(block):
            keep_left(unit, block, lf[unit, block])

    def prepare_right(m, unit):
        @pl.loop(m * CS, (m + 1) * CS)
        def _(block):
            keep_right(unit, block, rf[unit, block])

    def gather(step):
        def level(m, number, waits):
            for role in waits:
                left.arrived(m, role)
                right.arrived(m, role)
            for one in left.sends(m, number) + right.sends(m, number) + [share(m, role) for role in waits]:
                one.start()

        def prepare(m, waits):
            for role in waits:
                prepare_left(m, role)
                prepare_right(m, units_r[role])

        for m in range(CHUNKS):
            level(m, 1, (1, 2, 3))

        @pl.loop(0, SLOTS)
        def _(block):
            value = xs[block]
            keep_left(units_l[0], block, value)
            keep_right(units_r[0], block, value)

        for m in range(CHUNKS):
            prepare(m, (1, 2, 3))
            shared(m, 0)
            prepare_right(m, units_s[0])
        for m in range(CHUNKS):
            level(m, 2, (4, 5, 6))
            for role in (1, 2, 3):
                shared(m, role)
                prepare_right(m, units_s[role])
        for m in range(CHUNKS):
            prepare(m, (4, 5, 6))
            left.arrived(m, 7)
            right.arrived(m, 7)
            share(m, 7).start()
            prepare(m, (7,))
            for role in (4, 5, 6):
                shared(m, role)
                prepare_right(m, units_s[role])
        for m in range(CHUNKS):
            shared(m, 7)
            prepare_right(m, units_s[7])
            for number in range(3):
                for one in left.sends(m, number) + right.sends(m, number):
                    one.wait_send()
            for role in range(8):
                share(m, role).wait_send()

            @pl.when(step < STEPS - 1)
            def _():
                for device in neighbours:
                    pl.semaphore_signal(credit.at[m], inc=1, device_id=device, device_id_type=MESH)

    diagonal = lax.broadcasted_iota(jnp.int32, (BLK, BLK), 0) == lax.broadcasted_iota(jnp.int32, (BLK, BLK), 1)

    def trace_terms(value, weight):
        kept = jnp.where(diagonal, value, 0.0)
        return jnp.sum(kept.reshape(BLK // 8, 8, BLK), axis=0) * weight

    def multiply(step, m):
        @pl.loop(m * CS, (m + 1) * CS)
        def _(target):
            acc[...] = jnp.zeros_like(acc)

            @pl.loop(0, DEPTH // GROUP)
            def _(turn):
                first = turn * GROUP
                lhs = jnp.concatenate([ls[table[target, first + i]] for i in range(GROUP)], axis=1)
                rhs = jnp.concatenate([rs[table[target, DEPTH + first + i]] for i in range(GROUP)], axis=0)
                acc[...] += jnp.dot(lhs, rhs, preferred_element_type=jnp.float32)

            squared = acc[0:BLK, 0:BLK] + (
                acc[0:BLK, BLK : 2 * BLK] + acc[BLK : 2 * BLK, 0:BLK] + acc[BLK : 2 * BLK, BLK : 2 * BLK]
            )
            stored = xs[target]
            weight = table[SLOTS, target].astype(jnp.float32)
            tr[2 * step] += trace_terms(stored, weight)
            tr[2 * step + 1] += trace_terms(squared, weight)
            xs[target] = coef[step, 0] * stored + coef[step, 1] * squared

    for m in range(CHUNKS):
        remote = copy(x_hbm.at[part(m)], xs.at[part(m)], sw_s.at[m], sw_r.at[m], partner)
        local = pltpu.make_async_copy(x_hbm.at[part(m)], xs.at[part(m)], sw_r.at[m])
        pl.when(moved)(remote.start)
        pl.when(jnp.logical_not(moved))(local.start)
    tr[...] = jnp.zeros_like(tr)
    ls[COLS * SLOTS] = jnp.zeros((2 * BLK, BLK), jnp.bfloat16)
    for m in range(CHUNKS):
        remote = copy(x_hbm.at[part(m)], xs.at[part(m)], sw_s.at[m], sw_r.at[m], partner)
        local = pltpu.make_async_copy(x_hbm.at[part(m)], xs.at[part(m)], sw_r.at[m])
        pl.when(moved)(remote.wait)
        pl.when(jnp.logical_not(moved))(local.wait)
        send_own(m)

    def finals(m):
        remote = copy(xs.at[part(m)], out_hbm.at[part(m)], fin_s.at[m], fin_r.at[m], partner)
        local = pltpu.make_async_copy(xs.at[part(m)], out_hbm.at[part(m)], fin_r.at[m])
        return remote, local

    @pl.loop(0, STEPS)
    def _(step):
        gather(step)
        for m in range(CHUNKS):
            multiply(step, m)

            @pl.when(step < STEPS - 1)
            def _():
                pl.semaphore_wait(credit.at[m], len(neighbours))
                send_own(m)

            @pl.when(step == STEPS - 1)
            def _():
                remote, local = finals(m)
                pl.when(moved)(remote.start)
                pl.when(jnp.logical_not(moved))(local.start)

    for m in range(CHUNKS):
        remote, local = finals(m)
        pl.when(moved)(remote.wait)
        pl.when(jnp.logical_not(moved))(local.wait)


def run(table, coef, blocks):
    dma = pltpu.SemaphoreType.DMA
    anywhere = pl.BlockSpec(memory_space=pl.ANY)
    scalars = pl.BlockSpec(memory_space=pltpu.SMEM)
    return pl.pallas_call(
        kernel,
        out_shape=(
            jax.ShapeDtypeStruct((SLOTS, BLK, BLK), jnp.float32),
            jax.ShapeDtypeStruct((2 * STEPS, 8, BLK), jnp.float32),
        ),
        in_specs=[scalars, scalars, anywhere],
        out_specs=(anywhere, pl.BlockSpec(memory_space=pltpu.VMEM)),
        scratch_shapes=[
            pltpu.VMEM((SLOTS, BLK, BLK), jnp.float32),
            pltpu.VMEM((COLS, SLOTS, BLK, BLK), jnp.float32),
            pltpu.VMEM((ROWS, SLOTS, BLK, BLK), jnp.float32),
            pltpu.VMEM((COLS * SLOTS + 1, 2 * BLK, BLK), jnp.bfloat16),
            pltpu.VMEM((ROWS * SLOTS, BLK, 2 * BLK), jnp.bfloat16),
            pltpu.VMEM((2 * BLK, 2 * BLK), jnp.float32),
            dma((CHUNKS, 7)),
            dma((CHUNKS, 15)),
            dma((CHUNKS, 7)),
            dma((CHUNKS, 15)),
            dma((CHUNKS,)),
            dma((CHUNKS,)),
            dma((CHUNKS,)),
            dma((CHUNKS,)),
            pltpu.SemaphoreType.REGULAR((CHUNKS,)),
        ],
        compiler_params=pltpu.CompilerParams(
            collective_id=0, has_side_effects=True, vmem_limit_bytes=52 * 2**20
        ),
        cost_estimate=pl.CostEstimate(
            flops=STEPS * SLOTS * DEPTH * 8 * BLK**3, bytes_accessed=2 * SLOTS * BLK * BLK * 4, transcendentals=0
        ),
    )(table, coef, blocks)


def product_table(left_ids, right_ids, target_ids):
    count = target_ids.shape[0]
    order = jnp.arange(count, dtype=jnp.int32)
    same = (target_ids[:, None] == target_ids[None, :]) & (order[None, :] < order[:, None])
    place = target_ids * DEPTH + jnp.sum(same.astype(jnp.int32), axis=1)
    chosen = place[:, None] == jnp.arange(SLOTS * DEPTH, dtype=jnp.int32)[None, :]
    lefts = jnp.sum(jnp.where(chosen, left_ids[:, None] - COLS * SLOTS, 0), axis=0) + COLS * SLOTS
    rights = jnp.sum(jnp.where(chosen, right_ids[:, None], 0), axis=0)
    return jnp.concatenate([lefts.reshape(SLOTS, DEPTH), rights.reshape(SLOTS, DEPTH)], axis=1)


def partners():
    pairs = []
    for row in range(ROWS):
        for col in range(COLS):
            z, p = row % 4, col % 2
            here = row * COLS + col
            if p != zbits(z)[0]:
                pairs.append((here, (row - z + z + 1 - 2 * (z % 2)) * COLS + col + 1 - 2 * p))
            else:
                pairs.append((here, here))
    return pairs


def body(x_tiles, block_rows, block_cols, pair_left, pair_right, pair_target, branches):
    side_blocks = ROWS * BR
    is_diagonal = (block_rows[0, 0] == block_cols[0, 0]) & (block_rows[0, 0] < side_blocks)
    flags = jnp.pad(is_diagonal.astype(jnp.int32), (0, 2 * DEPTH - SLOTS))
    table = jnp.concatenate([product_table(pair_left[0, 0], pair_right[0, 0], pair_target[0, 0]), flags[None]], axis=0)
    table = lax.ppermute(table, ("row", "col"), partners())
    taken = (branches == 1).astype(jnp.float32)
    coef = jnp.stack([2.0 - 2.0 * taken, 2.0 * taken - 1.0], axis=1)
    purified, terms = run(table, coef, x_tiles[0, 0])
    sums = lax.psum(jnp.sum(terms, axis=(1, 2)), ("row", "col"))
    return (purified[None, None], sums.reshape(STEPS, 2) * (1.0 / (side_blocks * BLK)))


def solution(mesh):
    placed = (
        P("row", "col", None, None, None),
        P("row", "col", None),
        P("row", "col", None),
        P("row", "col", None),
        P("row", "col", None),
        P("row", "col", None),
        P(),
    )
    return jax.shard_map(
        body,
        mesh=mesh,
        in_specs=placed,
        out_specs=(P("row", "col", None, None, None), P()),
        check_vma=False,
    )
```

time: 1100 us -> 312 us (0.28)
  waiting for transfers between devices: 515 us -> 1.03 us
  Pallas kernels: 0 us -> 234 us
  local copies, waits for them, and re-layouts: 237 us -> 4.42 us
  matrix products: 191 us -> 0 us
  other arithmetic: 56.4 us -> 1.47 us
  between operations: 17.9 us -> 0.71 us
  loops' own time: 11.4 us -> 0 us
    all_gather x8 -> x0, waiting for transfers between devices: 512 us -> none  [the longest x4 369 us: body(): strip_right = lax.all_gather(stored, 'row', axis=0, tiled=True)]
    pallas_call x0 -> x1, Pallas kernels: none -> 234 us  [run(): pl.pallas_call(kernel, out_shape=(jax.ShapeDtypeStruct((SLOTS, BLK, BLK),...]
    dot_general x24 -> x0, matrix products: 191 us -> none  [the longest x12 122 us: slot_products(): jnp.einsum('pij,pjk->pik', left_blocks, right_blocks, precision=lax.Preci...]
    gather x32 -> x0, local copies, waits for them, and re-layouts: 186 us -> none  [the longest x12 96.4 us: slot_products(): right_blocks = jnp.take(strip_right, right_ids, axis=0)]
    select_n x3 -> x0, other arithmetic: 36 us -> none  [body(): jnp.where(branches[step_index] == 1, squared, 2.0 * stored - squared)]
    while x4 -> x0, local copies, waits for them, and re-layouts: 18.5 us -> none  [grouped_products(): return lax.fori_loop(0, rounds, one_round, empty)]
    select_n x3 -> x0, local copies, waits for them, and re-layouts: 18.1 us -> none  [body(): jnp.where(branches[step_index] == 1, squared, 2.0 * stored - squared)]
    broadcast_in_dim x1, other arithmetic: 11.9 us -> 0.01 us  [body(): flags[None]]
  transfers between devices with their start and end apart: 8 -> 1, of which waited for: 8 -> 1; matrix products, arithmetic and copies ran while one was open for 2% -> 0% of each run, Pallas kernels for 0% -> 0%
where the time goes in v1:
time: 312 us
  Pallas kernels  234 us (75%)
  blocking collectives  65.6 us (21%)
  starting transfers between devices  4.93 us (2%)
  local copies, waits for them, and re-layouts  4.42 us (1%)
    pallas_call x1, Pallas kernels, run(): pl.pallas_call(kernel, out_shape=(jax.ShapeDtypeStruct((SLOTS, BLK, BLK),...  234 us
    psum x1, blocking collectives, body(): sums = lax.psum(jnp.sum(terms, axis=(1, 2)), ('row', 'col'))  65.6 us
  transfers between devices with their start and end apart: 1, of which 1 were waited for; matrix products, arithmetic and copies ran while one was open for 0% of the time, Pallas kernels for 0%

profile of v1, /device:TPU:1, one launch (start us, length us, event | category | flops | bytes accessed | tf_op | source)
XLA Modules:
  0.0 311.7 jit_solution(18376749366962137745)
XLA Ops:
  0.6 0.0 copy-start.2
  0.6 0.7 and_bitcast_fusion
  1.3 0.0 copy-done.2
  1.4 0.2 convert_reduce_fusion
  1.6 0.0 copy-start.1
  1.6 0.7 copy-done.1
  2.3 0.7 copy-done.3
  3.0 0.2 select_reduce_fusion.1
  3.2 0.1 add.30
  3.2 0.1 reshape.40
  3.3 0.1 pad_add_fusion
  3.4 4.9 %collective-permute-start = (s32[13,64]{1,0:T(8,128)S(1)}, s32[13,64]{1,0:T(8,128)S(1)}, u32[]{:S(2)}, u32[]{:S(2)}) collective-permute-start(s32[13,64]{1,0:T(8,128)S(1)} %pad_add_fusion), channel_id=1, source_target_pairs={{0,0},{1,8},{2,2},{3,10},{4,4},{5,12},{6,6},{7,14},{8,1},{9,9},{10... | collective-permute-start | bytes 9992 | tf_op jit(solution)/shard_map/ppermute | solution.py:339
  8.3 0.0 copy-done.4
  8.4 0.1 copy.15
  8.5 0.1 copy.16
  8.5 0.1 pad_maximum_fusion.coef
  8.6 1.0 collective-permute-done.table
  9.7 1.1 copy-done
  10.8 233.5 %shard_map.86 = (f32[12,128,128]{2,1,0:T(8,128)S(1)}, f32[8,8,128]{2,1,0:T(8,128)S(1)}) custom-call(s32[13,64]{1,0:T(8,128)S(1)} %collective-permute-done.table, f32[4,2]{1,0:T(4,128)S(1)} %pad_maximum_fusion.coef, f32[12,128,128]{2,1,0:T(8,128)S(1)} %bitcast.11), custom_call_target="tpu_custom_call" | custom-call | flops 25769803776 | bytes 1572864 | tf_op jit(solution)/shard_map/pallas_call | solution.py:276
  244.3 0.1 reduce_sum.39
  244.5 65.6 %psum.7 = f32[8]{0:T(128)S(1)} all-reduce(f32[8]{0:T(128)S(1)} %reduce_sum.39), channel_id=1, replica_groups=mesh['row'=16,'col'=8] {'row','col'}, use_global_device_ids=true, to_apply=%region_4.5 | all-reduce | flops 8 | bytes 64 | tf_op jit(solution)/shard_map/psum | solution.py:343
  310.1 0.1 mul.24
  310.2 0.7 copy.17
  310.8 0.9 copy.19
  (11 shorter events, 0.1 us)
Async XLA Ops:
  0.6 0.7 copy-start.2
  1.6 0.7 copy-start.1
  2.3 0.7 copy-start.3
  3.3 5.0 %copy-start.4 = (s32[4]{0:T(128)S(1)}, s32[4]{0:T(128)}, u32[]{:S(2)}) copy-start(s32[4]{0:T(128)} %param.13) | copy-start | bytes 52
  3.4 6.3 %collective-permute-start = (s32[13,64]{1,0:T(8,128)S(1)}, s32[13,64]{1,0:T(8,128)S(1)}, u32[]{:S(2)}, u32[]{:S(2)}) collective-permute-start(s32[13,64]{1,0:T(8,128)S(1)} %pad_add_fusion), channel_id=1, source_target_pairs={{0,0},{1,8},{2,2},{3,10},{4,4},{5,12},{6,6},{7,14},{8,1},{9,9},{10... | collective-permute-start | bytes 9992 | tf_op jit(solution)/shard_map/ppermute | solution.py:339
  9.7 1.1 copy-start

commit v2 on v1

--- a/solution.py
+++ b/solution.py
@@ -24,7 +24,10 @@
     return low, high
 
 
-def kernel(table, coef, x_hbm, out_hbm, tr, xs, lf, rf, ls, rs, acc, r_l, r_r, s_l, s_r, sw_s, sw_r, fin_s, fin_r, credit):
+def kernel(
+    table, coef, x_hbm, out_hbm, traces, xs, lf, rf, ls, rs, acc, terms, sums, heard,
+    r_l, r_r, s_l, s_r, sw_s, sw_r, fin_s, fin_r, t_s, t_r, credit,
+):
     row = lax.axis_index("row")
     col = lax.axis_index("col")
     x, z, y, p = row // 4, row % 4, col // 2, col % 2
@@ -42,6 +45,16 @@
     r_prev = (((x + 3) % 4) * 4 + z, col)
     r_pair = (x * 4 + z_high, col)
     neighbours = (l_next, l_prev, l_pair, r_next, r_prev, r_pair, sibling)
+
+    pairs = (
+        (row, (y + 1 - 2 * (y % 2)) * 2 + p),
+        (row, (3 - y) * 2 + p),
+        l_pair,
+        r_pair,
+        ((x + 1 - 2 * (x % 2)) * 4 + z, col),
+        ((3 - x) * 4 + z, col),
+        sibling,
+    )
 
     barrier = pltpu.get_barrier_semaphore()
     for device in neighbours + (partner,):
@@ -146,6 +159,29 @@
         def _(block):
             keep_right(unit, block, rf[unit, block])
 
+    diagonal = lax.broadcasted_iota(jnp.int32, (BLK, BLK), 0) == lax.broadcasted_iota(jnp.int32, (BLK, BLK), 1)
+
+    def folded(value):
+        return jnp.sum(value.reshape(BLK // 8, 8, BLK), axis=0)
+
+    def total(step, stage):
+        def exchange(index):
+            return copy(sums.at[index], heard.at[index], t_s.at[index], t_r.at[index], pairs[index])
+
+        @pl.when(step == STEPS - 1)
+        def _():
+            if 0 < stage <= len(pairs):
+                exchange(stage - 1).wait()
+                sums[stage] = sums[stage - 1] + heard[stage - 1]
+            if stage < len(pairs):
+                exchange(stage).start()
+            if stage == len(pairs):
+                found = sums[stage]
+                for at in range(STEPS):
+                    for which in range(2):
+                        place = 2 * at + which
+                        traces[at, which] = jnp.sum(found[place : place + 1]) * (1.0 / (ROWS * BR * BLK))
+
     def gather(step):
         def level(m, number, waits):
             for role in waits:
@@ -162,18 +198,29 @@
         for m in range(CHUNKS):
             level(m, 1, (1, 2, 3))
 
+        terms[...] = jnp.zeros_like(terms)
+
         @pl.loop(0, SLOTS)
         def _(block):
             value = xs[block]
             keep_left(units_l[0], block, value)
             keep_right(units_r[0], block, value)
+            weight = table[SLOTS, block].astype(jnp.float32)
+            terms[0] += folded(jnp.where(diagonal, value, 0.0)) * weight
+            terms[1] += folded(value * value)
+
+        for which in range(2):
+            sums[0, pl.ds(2 * step + which, 1)] = jnp.sum(terms[which], axis=0, keepdims=True)
+        total(step, 0)
 
         for m in range(CHUNKS):
             prepare(m, (1, 2, 3))
+            total(step, 1 + m)
             shared(m, 0)
             prepare_right(m, units_s[0])
         for m in range(CHUNKS):
             level(m, 2, (4, 5, 6))
+            total(step, 5 + m)
             for role in (1, 2, 3):
                 shared(m, role)
                 prepare_right(m, units_s[role])
@@ -200,12 +247,6 @@
                 for device in neighbours:
                     pl.semaphore_signal(credit.at[m], inc=1, device_id=device, device_id_type=MESH)
 
-    diagonal = lax.broadcasted_iota(jnp.int32, (BLK, BLK), 0) == lax.broadcasted_iota(jnp.int32, (BLK, BLK), 1)
-
-    def trace_terms(value, weight):
-        kept = jnp.where(diagonal, value, 0.0)
-        return jnp.sum(kept.reshape(BLK // 8, 8, BLK), axis=0) * weight
-
     def multiply(step, m):
         @pl.loop(m * CS, (m + 1) * CS)
         def _(target):
@@ -222,9 +263,6 @@
                 acc[0:BLK, BLK : 2 * BLK] + acc[BLK : 2 * BLK, 0:BLK] + acc[BLK : 2 * BLK, BLK : 2 * BLK]
             )
             stored = xs[target]
-            weight = table[SLOTS, target].astype(jnp.float32)
-            tr[2 * step] += trace_terms(stored, weight)
-            tr[2 * step + 1] += trace_terms(squared, weight)
             xs[target] = coef[step, 0] * stored + coef[step, 1] * squared
 
     for m in range(CHUNKS):
@@ -232,7 +270,7 @@
         local = pltpu.make_async_copy(x_hbm.at[part(m)], xs.at[part(m)], sw_r.at[m])
         pl.when(moved)(remote.start)
         pl.when(jnp.logical_not(moved))(local.start)
-    tr[...] = jnp.zeros_like(tr)
+    sums[...] = jnp.zeros_like(sums)
     ls[COLS * SLOTS] = jnp.zeros((2 * BLK, BLK), jnp.bfloat16)
     for m in range(CHUNKS):
         remote = copy(x_hbm.at[part(m)], xs.at[part(m)], sw_s.at[m], sw_r.at[m], partner)
@@ -277,10 +315,10 @@
         kernel,
         out_shape=(
             jax.ShapeDtypeStruct((SLOTS, BLK, BLK), jnp.float32),
-            jax.ShapeDtypeStruct((2 * STEPS, 8, BLK), jnp.float32),
+            jax.ShapeDtypeStruct((STEPS, 2), jnp.float32),
         ),
         in_specs=[scalars, scalars, anywhere],
-        out_specs=(anywhere, pl.BlockSpec(memory_space=pltpu.VMEM)),
+        out_specs=(anywhere, scalars),
         scratch_shapes=[
             pltpu.VMEM((SLOTS, BLK, BLK), jnp.float32),
             pltpu.VMEM((COLS, SLOTS, BLK, BLK), jnp.float32),
@@ -288,6 +326,9 @@
             pltpu.VMEM((COLS * SLOTS + 1, 2 * BLK, BLK), jnp.bfloat16),
             pltpu.VMEM((ROWS * SLOTS, BLK, 2 * BLK), jnp.bfloat16),
             pltpu.VMEM((2 * BLK, 2 * BLK), jnp.float32),
+            pltpu.VMEM((2, 8, BLK), jnp.float32),
+            pltpu.VMEM((8, 8, BLK), jnp.float32),
+            pltpu.VMEM((7, 8, BLK), jnp.float32),
             dma((CHUNKS, 7)),
             dma((CHUNKS, 15)),
             dma((CHUNKS, 7)),
@@ -296,6 +337,8 @@
             dma((CHUNKS,)),
             dma((CHUNKS,)),
             dma((CHUNKS,)),
+            dma((7,)),
+            dma((7,)),
             pltpu.SemaphoreType.REGULAR((CHUNKS,)),
         ],
         compiler_params=pltpu.CompilerParams(
@@ -339,9 +382,8 @@
     table = lax.ppermute(table, ("row", "col"), partners())
     taken = (branches == 1).astype(jnp.float32)
     coef = jnp.stack([2.0 - 2.0 * taken, 2.0 * taken - 1.0], axis=1)
-    purified, terms = run(table, coef, x_tiles[0, 0])
-    sums = lax.psum(jnp.sum(terms, axis=(1, 2)), ("row", "col"))
-    return (purified[None, None], sums.reshape(STEPS, 2) * (1.0 / (side_blocks * BLK)))
+    purified, traces = run(table, coef, x_tiles[0, 0])
+    return (purified[None, None], traces)
 
 
 def solution(mesh):

time: 312 us -> 261 us (0.84)
  blocking collectives: 65.6 us -> 0 us
  Pallas kernels: 234 us -> 248 us
    psum x1 -> x0, blocking collectives: 65.6 us -> none  [body(): sums = lax.psum(jnp.sum(terms, axis=(1, 2)), ('row', 'col'))]
    pallas_call x1, Pallas kernels: 234 us -> 248 us  [run(): pl.pallas_call(kernel, out_shape=(jax.ShapeDtypeStruct((SLOTS, BLK, BLK),...]
where the time goes in v2:
time: 261 us
  Pallas kernels  248 us (95%)
  starting transfers between devices  4.93 us (2%)
  local copies, waits for them, and re-layouts  4.33 us (2%)
    pallas_call x1, Pallas kernels, run(): pl.pallas_call(kernel, out_shape=(jax.ShapeDtypeStruct((SLOTS, BLK, BLK),...  248 us
  transfers between devices with their start and end apart: 1, of which 1 were waited for; matrix products, arithmetic and copies ran while one was open for 0% of the time, Pallas kernels for 0%

profile of v2, /device:TPU:1, one launch (start us, length us, event | category | flops | bytes accessed | tf_op | source)
XLA Modules:
  0.0 260.5 jit_solution(16671748661965355904)
XLA Ops:
  0.6 0.0 copy-start.2
  0.6 0.7 and_bitcast_fusion
  1.3 0.0 copy-done.2
  1.4 0.2 convert_reduce_fusion
  1.6 0.0 copy-start.1
  1.6 0.7 copy-done.1
  2.3 0.0 copy-start.3
  2.3 0.7 copy-done.3
  3.0 0.2 select_reduce_fusion.1
  3.2 0.1 add.28
  3.2 0.1 reshape.37
  3.3 0.0 copy-start.4
  3.3 0.1 pad_add_fusion
  3.4 4.9 %collective-permute-start = (s32[13,64]{1,0:T(8,128)S(1)}, s32[13,64]{1,0:T(8,128)S(1)}, u32[]{:S(2)}, u32[]{:S(2)}) collective-permute-start(s32[13,64]{1,0:T(8,128)S(1)} %pad_add_fusion), channel_id=1, source_target_pairs={{0,0},{1,8},{2,2},{3,10},{4,4},{5,12},{6,6},{7,14},{8,1},{9,9},{10... | collective-permute-start | bytes 9992 | tf_op jit(solution)/shard_map/ppermute | solution.py:382
  8.3 0.0 copy-done.4
  8.4 0.1 copy.12
  8.5 0.1 copy.13
  8.5 0.1 pad_maximum_fusion.coef
  8.6 1.0 collective-permute-done.table
  9.7 0.0 copy-start
  9.7 1.1 copy-done
  10.8 248.2 %shard_map.86 = (f32[12,128,128]{2,1,0:T(8,128)S(1)}, f32[4,2]{1,0:T(4,128)S(1)}) custom-call(s32[13,64]{1,0:T(8,128)S(1)} %collective-permute-done.table, f32[4,2]{1,0:T(4,128)S(1)} %pad_maximum_fusion.coef, f32[12,128,128]{2,1,0:T(8,128)S(1)} %bitcast.11), custom_call_target="tpu_custom_call" | custom-call | flops 25769803776 | bytes 1572864 | tf_op jit(solution)/shard_map/pallas_call | solution.py:314
  259.0 0.6 copy.14
  259.6 0.9 copy.16
  (7 shorter events, 0.1 us)
Async XLA Ops:
  0.6 0.7 copy-start.2
  1.6 0.7 copy-start.1
  2.3 0.7 copy-start.3
  3.3 5.0 %copy-start.4 = (s32[4]{0:T(128)S(1)}, s32[4]{0:T(128)}, u32[]{:S(2)}) copy-start(s32[4]{0:T(128)} %param.13) | copy-start | bytes 52
  3.4 6.3 %collective-permute-start = (s32[13,64]{1,0:T(8,128)S(1)}, s32[13,64]{1,0:T(8,128)S(1)}, u32[]{:S(2)}, u32[]{:S(2)}) collective-permute-start(s32[13,64]{1,0:T(8,128)S(1)} %pad_add_fusion), channel_id=1, source_target_pairs={{0,0},{1,8},{2,2},{3,10},{4,4},{5,12},{6,6},{7,14},{8,1},{9,9},{10... | collective-permute-start | bytes 9992 | tf_op jit(solution)/shard_map/ppermute | solution.py:382
  9.7 1.1 copy-start

commit v3 on v2

--- a/solution.py
+++ b/solution.py
@@ -13,9 +13,9 @@
 ROWS = 16
 COLS = 8
 DEPTH = 32
-CHUNKS = 4
+CHUNKS = 6
 CS = SLOTS // CHUNKS
-GROUP = 8
+RELAYED = 2
 
 
 def zbits(z):
@@ -25,7 +25,7 @@
 
 
 def kernel(
-    table, coef, x_hbm, out_hbm, traces, xs, lf, rf, ls, rs, acc, terms, sums, heard,
+    table, coef, x_hbm, out_hbm, traces, xs, lf, rf, ls, rs, terms, sums, heard,
     r_l, r_r, s_l, s_r, sw_s, sw_r, fin_s, fin_r, t_s, t_r, credit,
 ):
     row = lax.axis_index("row")
@@ -73,6 +73,9 @@
     def part(m):
         return pl.ds(m * CS, CS)
 
+    def by_core(zero, one):
+        return zero + p * (one - zero)
+
     def copy(src, dst, ssem, rsem, device):
         return pltpu.make_async_remote_copy(
             src_ref=src, dst_ref=dst, send_sem=ssem, recv_sem=rsem, device_id=device, device_id_type=MESH
@@ -83,35 +86,30 @@
             self.buf, self.units, self.rsem, self.ssem = buf, units, rsem, ssem
             self.nxt, self.prv, self.pair = nxt, prv, pair
 
-        def source(self, role, m):
-            return xs.at[part(m)] if role == 0 else self.buf.at[self.units[role], part(m)]
-
         def plan(self, m):
             nxt, prv, pair = self.nxt, self.prv, self.pair
             first = [(0, nxt, 1), (0, prv, 2), (0, pair, 3)]
             second = [(1, nxt, 4)] if m % 2 == 0 else [(2, prv, 4)]
-            if m < CHUNKS // 2:
-                second += [(1, pair, 5), (2, pair, 6)]
-                third = [(4, pair, 7)]
+            relay = ([(1, pair, 5), (2, pair, 6)], [(4, pair, 7)])
+            onward = ([(3, nxt, 5), (3, prv, 6)], [(5, nxt, 7)] if m % 2 == 0 else [(6, prv, 7)])
+            unit = lambda sends: [(self.units[role], device, there) for role, device, there in sends]
+            if m == RELAYED:
+                more = [
+                    [(by_core(c, d), (by_core(e[0], f[0]), by_core(e[1], f[1])), there) for (c, e, there), (d, f, _) in both]
+                    for both in (zip(unit(onward[0]), unit(relay[0])), zip(unit(onward[1]), unit(relay[1])))
+                ]
             else:
-                second += [(3, nxt, 5), (3, prv, 6)]
-                third = [(5, nxt, 7)] if m % 2 == 0 else [(6, prv, 7)]
-            return first, second, third
+                more = [unit(sends) for sends in (relay if m < RELAYED else onward)]
+            return unit(first), unit(second) + more[0], more[1]
 
         def sends(self, m, level):
             plan = self.plan(m)
             at = sum(len(one) for one in plan[:level])
             made = []
-            for index, (role, device, there) in enumerate(plan[level]):
-                made.append(
-                    copy(
-                        self.source(role, m),
-                        self.buf.at[self.units[role], part(m)],
-                        self.ssem.at[m, at + index],
-                        self.rsem.at[m, there - 1],
-                        device,
-                    )
-                )
+            for index, (unit, device, there) in enumerate(plan[level]):
+                place = self.buf.at[unit, part(m)]
+                source = xs.at[part(m)] if level == 0 else place
+                made.append(copy(source, place, self.ssem.at[m, at + index], self.rsem.at[m, there - 1], device))
             return made
 
         def arrived(self, m, role):
@@ -123,7 +121,7 @@
 
     def share(m, role):
         place = rf.at[units_r[role], part(m)]
-        return copy(right.source(role, m), place, s_r.at[m, 7 + role], r_r.at[m, 7 + role], sibling)
+        return copy(xs.at[part(m)] if role == 0 else place, place, s_r.at[m, 7 + role], r_r.at[m, 7 + role], sibling)
 
     def shared(m, role):
         place = rf.at[units_s[role], part(m)]
@@ -197,7 +195,47 @@
 
         for m in range(CHUNKS):
             level(m, 1, (1, 2, 3))
-
+            if m == 0:
+                prepare_own(step)
+            prepare(m, (1, 2, 3))
+            shared(m, 0)
+            prepare_right(m, units_s[0])
+        for m in range(CHUNKS):
+            level(m, 2, (4, 5, 6))
+            for role in (1, 2, 3):
+                shared(m, role)
+                prepare_right(m, units_s[role])
+            prepare(m, (4, 5, 6))
+        for m in range(CHUNKS):
+            left.arrived(m, 7)
+            right.arrived(m, 7)
+            share(m, 7).start()
+            prepare(m, (7,))
+            for role in (4, 5, 6):
+                shared(m, role)
+                prepare_right(m, units_s[role])
+            if m > 0:
+                last_share(m - 1)
+                finish(step, m - 1)
+        last_share(CHUNKS - 1)
+
+    def last_share(m):
+        shared(m, 7)
+        prepare_right(m, units_s[7])
+
+    def finish(step, m):
+        for number in range(3):
+            for one in left.sends(m, number) + right.sends(m, number):
+                one.wait_send()
+        for role in range(8):
+            share(m, role).wait_send()
+
+        @pl.when(step < STEPS - 1)
+        def _():
+            for device in neighbours:
+                pl.semaphore_signal(credit.at[m], inc=1, device_id=device, device_id_type=MESH)
+
+    def prepare_own(step):
         terms[...] = jnp.zeros_like(terms)
 
         @pl.loop(0, SLOTS)
@@ -211,56 +249,15 @@
 
         for which in range(2):
             sums[0, pl.ds(2 * step + which, 1)] = jnp.sum(terms[which], axis=0, keepdims=True)
-        total(step, 0)
-
-        for m in range(CHUNKS):
-            prepare(m, (1, 2, 3))
-            total(step, 1 + m)
-            shared(m, 0)
-            prepare_right(m, units_s[0])
-        for m in range(CHUNKS):
-            level(m, 2, (4, 5, 6))
-            total(step, 5 + m)
-            for role in (1, 2, 3):
-                shared(m, role)
-                prepare_right(m, units_s[role])
-        for m in range(CHUNKS):
-            prepare(m, (4, 5, 6))
-            left.arrived(m, 7)
-            right.arrived(m, 7)
-            share(m, 7).start()
-            prepare(m, (7,))
-            for role in (4, 5, 6):
-                shared(m, role)
-                prepare_right(m, units_s[role])
-        for m in range(CHUNKS):
-            shared(m, 7)
-            prepare_right(m, units_s[7])
-            for number in range(3):
-                for one in left.sends(m, number) + right.sends(m, number):
-                    one.wait_send()
-            for role in range(8):
-                share(m, role).wait_send()
-
-            @pl.when(step < STEPS - 1)
-            def _():
-                for device in neighbours:
-                    pl.semaphore_signal(credit.at[m], inc=1, device_id=device, device_id_type=MESH)
 
     def multiply(step, m):
         @pl.loop(m * CS, (m + 1) * CS)
         def _(target):
-            acc[...] = jnp.zeros_like(acc)
-
-            @pl.loop(0, DEPTH // GROUP)
-            def _(turn):
-                first = turn * GROUP
-                lhs = jnp.concatenate([ls[table[target, first + i]] for i in range(GROUP)], axis=1)
-                rhs = jnp.concatenate([rs[table[target, DEPTH + first + i]] for i in range(GROUP)], axis=0)
-                acc[...] += jnp.dot(lhs, rhs, preferred_element_type=jnp.float32)
-
-            squared = acc[0:BLK, 0:BLK] + (
-                acc[0:BLK, BLK : 2 * BLK] + acc[BLK : 2 * BLK, 0:BLK] + acc[BLK : 2 * BLK, BLK : 2 * BLK]
+            lhs = jnp.concatenate([ls[table[target, i]] for i in range(DEPTH)], axis=1)
+            rhs = jnp.concatenate([rs[table[target, DEPTH + i]] for i in range(DEPTH)], axis=0)
+            found = jnp.dot(lhs, rhs, preferred_element_type=jnp.float32)
+            squared = found[0:BLK, 0:BLK] + (
+                found[0:BLK, BLK : 2 * BLK] + found[BLK : 2 * BLK, 0:BLK] + found[BLK : 2 * BLK, BLK : 2 * BLK]
             )
             stored = xs[target]
             xs[target] = coef[step, 0] * stored + coef[step, 1] * squared
@@ -287,8 +284,12 @@
     @pl.loop(0, STEPS)
     def _(step):
         gather(step)
+        total(step, 0)
         for m in range(CHUNKS):
             multiply(step, m)
+            if m == 0:
+                finish(step, CHUNKS - 1)
+            total(step, 1 + m)
 
             @pl.when(step < STEPS - 1)
             def _():
@@ -301,6 +302,7 @@
                 pl.when(moved)(remote.start)
                 pl.when(jnp.logical_not(moved))(local.start)
 
+    total(STEPS - 1, CHUNKS + 1)
     for m in range(CHUNKS):
         remote, local = finals(m)
         pl.when(moved)(remote.wait)
@@ -325,7 +327,6 @@
             pltpu.VMEM((ROWS, SLOTS, BLK, BLK), jnp.float32),
             pltpu.VMEM((COLS * SLOTS + 1, 2 * BLK, BLK), jnp.bfloat16),
             pltpu.VMEM((ROWS * SLOTS, BLK, 2 * BLK), jnp.bfloat16),
-            pltpu.VMEM((2 * BLK, 2 * BLK), jnp.float32),
             pltpu.VMEM((2, 8, BLK), jnp.float32),
             pltpu.VMEM((8, 8, BLK), jnp.float32),
             pltpu.VMEM((7, 8, BLK), jnp.float32),

time: 261 us -> 232 us (0.89)
  Pallas kernels: 248 us -> 219 us
    pallas_call x1, Pallas kernels: 248 us -> 219 us  [run(): pl.pallas_call(kernel, out_shape=(jax.ShapeDtypeStruct((SLOTS, BLK, BLK),...]
where the time goes in v3:
time: 232 us
  Pallas kernels  219 us (94%)
  starting transfers between devices  4.93 us (2%)
  local copies, waits for them, and re-layouts  4.33 us (2%)
    pallas_call x1, Pallas kernels, run(): pl.pallas_call(kernel, out_shape=(jax.ShapeDtypeStruct((SLOTS, BLK, BLK),...  219 us
    ppermute x1, starting transfers between devices, body(): table = lax.ppermute(table, ('row', 'col'), partners())  4.93 us
  transfers between devices with their start and end apart: 1, of which 1 were waited for; matrix products, arithmetic and copies ran while one was open for 0% of the time, Pallas kernels for 0%

profile of v3, /device:TPU:1, one launch (start us, length us, event | category | flops | bytes accessed | tf_op | source)
XLA Modules:
  0.0 231.7 jit_solution(10916733803335755075)
XLA Ops:
  0.6 0.0 copy-start.2
  0.6 0.7 and_bitcast_fusion
  1.3 0.0 copy-done.2
  1.4 0.2 convert_reduce_fusion
  1.6 0.0 copy-start.1
  1.6 0.7 copy-done.1
  2.3 0.0 copy-start.3
  2.3 0.7 copy-done.3
  3.0 0.2 select_reduce_fusion.1
  3.2 0.1 add.28
  3.2 0.1 reshape.37
  3.3 0.0 copy-start.4
  3.3 0.1 pad_add_fusion
  3.4 4.9 %collective-permute-start = (s32[13,64]{1,0:T(8,128)S(1)}, s32[13,64]{1,0:T(8,128)S(1)}, u32[]{:S(2)}, u32[]{:S(2)}) collective-permute-start(s32[13,64]{1,0:T(8,128)S(1)} %pad_add_fusion), channel_id=1, source_target_pairs={{0,0},{1,8},{2,2},{3,10},{4,4},{5,12},{6,6},{7,14},{8,1},{9,9},{10... | collective-permute-start | bytes 9992 | tf_op jit(solution)/shard_map/ppermute | solution.py:383
  8.3 0.0 copy-done.4
  8.4 0.1 copy.12
  8.5 0.1 copy.13
  8.5 0.1 pad_maximum_fusion.coef
  8.6 1.0 collective-permute-done.table
  9.7 0.0 copy-start
  9.7 1.1 copy-done
  10.8 219.4 %shard_map.86 = (f32[12,128,128]{2,1,0:T(8,128)S(1)}, f32[4,2]{1,0:T(4,128)S(1)}) custom-call(s32[13,64]{1,0:T(8,128)S(1)} %collective-permute-done.table, f32[4,2]{1,0:T(4,128)S(1)} %pad_maximum_fusion.coef, f32[12,128,128]{2,1,0:T(8,128)S(1)} %bitcast.11), custom_call_target="tpu_custom_call" | custom-call | flops 25769803776 | bytes 1572864 | tf_op jit(solution)/shard_map/pallas_call | solution.py:316
  230.2 0.6 copy.14
  230.9 0.9 copy.16
  (7 shorter events, 0.1 us)
Async XLA Ops:
  0.6 0.7 copy-start.2
  1.6 0.7 copy-start.1
  2.3 0.7 copy-start.3
  3.3 5.0 %copy-start.4 = (s32[4]{0:T(128)S(1)}, s32[4]{0:T(128)}, u32[]{:S(2)}) copy-start(s32[4]{0:T(128)} %param.13) | copy-start | bytes 52
  3.4 6.3 %collective-permute-start = (s32[13,64]{1,0:T(8,128)S(1)}, s32[13,64]{1,0:T(8,128)S(1)}, u32[]{:S(2)}, u32[]{:S(2)}) collective-permute-start(s32[13,64]{1,0:T(8,128)S(1)} %pad_add_fusion), channel_id=1, source_target_pairs={{0,0},{1,8},{2,2},{3,10},{4,4},{5,12},{6,6},{7,14},{8,1},{9,9},{10... | collective-permute-start | bytes 9992 | tf_op jit(solution)/shard_map/ppermute | solution.py:383
  9.7 1.1 copy-start

commit v4 on v3

--- a/solution.py
+++ b/solution.py
@@ -15,6 +15,7 @@
 DEPTH = 32
 CHUNKS = 6
 CS = SLOTS // CHUNKS
+VMEM_BYTES = 60 * 2**20
 RELAYED = 2
 
 
@@ -25,8 +26,8 @@
 
 
 def kernel(
-    table, coef, x_hbm, out_hbm, traces, xs, lf, rf, ls, rs, terms, sums, heard,
-    r_l, r_r, s_l, s_r, sw_s, sw_r, fin_s, fin_r, t_s, t_r, credit,
+    branches, rows_hbm, cols_hbm, left_hbm, right_hbm, target_hbm, x_hbm, out_hbm, traces, xs, lf, rf, ls, rs, rows_in, cols_in, left_in, right_in, target_in, lists, built, table, terms, sums, rings,
+    r_l, r_r, s_l, s_r, sw_s, sw_r, fin_s, fin_r, t_s, t_r, n_s, n_r, credit,
 ):
     row = lax.axis_index("row")
     col = lax.axis_index("col")
@@ -46,20 +47,17 @@
     r_pair = (x * 4 + z_high, col)
     neighbours = (l_next, l_prev, l_pair, r_next, r_prev, r_pair, sibling)
 
-    pairs = (
-        (row, (y + 1 - 2 * (y % 2)) * 2 + p),
-        (row, (3 - y) * 2 + p),
-        l_pair,
-        r_pair,
-        ((x + 1 - 2 * (x % 2)) * 4 + z, col),
-        ((3 - x) * 4 + z, col),
-        sibling,
+    along = (
+        (y, [(row, ((y + o) % 4) * 2 + p) for o in (1, 2, 3)]),
+        (z, [(x * 4 + (z + o) % 4, col) for o in (1, 2, 3)]),
+        (x, [(((x + o) % 4) * 4 + z, col) for o in (1, 2, 3)]),
     )
+    greeted = neighbours + (partner,) + tuple(devices[1] for _, devices in along)
 
     barrier = pltpu.get_barrier_semaphore()
-    for device in neighbours + (partner,):
+    for device in greeted:
         pl.semaphore_signal(barrier, inc=1, device_id=device, device_id_type=MESH)
-    pl.semaphore_wait(barrier, len(neighbours) + 1)
+    pl.semaphore_wait(barrier, len(greeted))
 
     def roles(q, h, unit):
         a, b, c = (q + 3) % 4, (q + 1) % 4, (q + 2) % 4
@@ -93,13 +91,18 @@
             relay = ([(1, pair, 5), (2, pair, 6)], [(4, pair, 7)])
             onward = ([(3, nxt, 5), (3, prv, 6)], [(5, nxt, 7)] if m % 2 == 0 else [(6, prv, 7)])
             unit = lambda sends: [(self.units[role], device, there) for role, device, there in sends]
-            if m == RELAYED:
-                more = [
-                    [(by_core(c, d), (by_core(e[0], f[0]), by_core(e[1], f[1])), there) for (c, e, there), (d, f, _) in both]
-                    for both in (zip(unit(onward[0]), unit(relay[0])), zip(unit(onward[1]), unit(relay[1])))
-                ]
-            else:
-                more = [unit(sends) for sends in (relay if m < RELAYED else onward)]
+            ways = [[unit(way[level]) for way in (onward, relay)] for level in range(2)]
+            more = []
+            for level, (on, back) in enumerate(ways):
+                if m == RELAYED or (level == 1 and m == CHUNKS - 1):
+                    more.append(
+                        [
+                            (by_core(c, d), (by_core(e[0], f[0]), by_core(e[1], f[1])), there)
+                            for (c, e, there), (d, f, _) in zip(on, back)
+                        ]
+                    )
+                else:
+                    more.append(back if m < RELAYED else on)
             return unit(first), unit(second) + more[0], more[1]
 
         def sends(self, m, level):
@@ -127,9 +130,14 @@
         place = rf.at[units_s[role], part(m)]
         copy(place, place, s_r.at[m, 0], r_r.at[m, 7 + role], sibling).wait_recv()
 
-    def send_own(m):
-        for one in left.sends(m, 0) + right.sends(m, 0) + [share(m, 0)]:
+    def send_own(m, first=False):
+        to_next, to_prev, to_pair = left.sends(m, 0)
+        for one in [to_next, to_prev] + right.sends(m, 0) + [share(m, 0)]:
             one.start()
+        if first:
+            pl.when(jnp.logical_not(moved))(to_pair.start)
+        else:
+            to_pair.start()
 
     def split(value):
         top = value.astype(jnp.bfloat16)
@@ -163,22 +171,84 @@
         return jnp.sum(value.reshape(BLK // 8, 8, BLK), axis=0)
 
     def total(step, stage):
-        def exchange(index):
-            return copy(sums.at[index], heard.at[index], t_s.at[index], t_r.at[index], pairs[index])
+        def core():
+            return copy(sums.at[0], sums.at[1], t_s.at[0, 0], t_r.at[0, 0], sibling)
+
+        def ring(index):
+            place, devices = along[index]
+            mine = rings.at[index, place]
+            return [copy(mine, mine, t_s.at[index + 1, o], t_r.at[index + 1, o], devices[o]) for o in range(3)]
 
         @pl.when(step == STEPS - 1)
         def _():
-            if 0 < stage <= len(pairs):
-                exchange(stage - 1).wait()
-                sums[stage] = sums[stage - 1] + heard[stage - 1]
-            if stage < len(pairs):
-                exchange(stage).start()
-            if stage == len(pairs):
-                found = sums[stage]
-                for at in range(STEPS):
-                    for which in range(2):
-                        place = 2 * at + which
-                        traces[at, which] = jnp.sum(found[place : place + 1]) * (1.0 / (ROWS * BR * BLK))
+            if stage == 0:
+                core().start()
+                return
+            if stage == 1:
+                core().wait()
+                found = sums[0] + sums[1]
+            else:
+                for one in ring(stage - 2):
+                    one.wait()
+                found = (rings[stage - 2, 0] + rings[stage - 2, 1]) + (rings[stage - 2, 2] + rings[stage - 2, 3])
+            if stage < 4:
+                rings[stage - 1, along[stage - 1][0]] = found
+                for one in ring(stage - 1):
+                    one.start()
+                return
+            for at in range(STEPS):
+                for which in range(2):
+                    place = 2 * at + which
+                    traces[which, at] = jnp.sum(found[place : place + 1]) * (1.0 / (ROWS * BR * BLK))
+
+    def lists_copies():
+        pairs = (
+            (rows_hbm, rows_in),
+            (cols_hbm, cols_in),
+            (left_hbm, left_in),
+            (right_hbm, right_in),
+            (target_hbm, target_in),
+        )
+        for at, (src, dst) in enumerate(pairs):
+            yield copy(src, dst, n_s.at[at], n_r.at[at], partner), pltpu.make_async_copy(src, dst, n_r.at[at])
+
+    def build_table():
+        for remote, local in lists_copies():
+            pl.when(moved)(remote.wait)
+            pl.when(jnp.logical_not(moved))(local.wait)
+        width = SLOTS * DEPTH
+        count = target_in.shape[1]
+        lists[...] = jnp.full_like(lists, SLOTS)
+        lists[0:1, 0:count] = left_in[...]
+        lists[1:2, 0:count] = right_in[...]
+        lists[2:3, 0:count] = target_in[...]
+        same = (rows_in[...] == cols_in[...]) & (rows_in[...] < ROWS * BR)
+        built[2:3, 0:SLOTS] = same.astype(jnp.int32)
+        given = lists[...]
+        lane = lax.broadcasted_iota(jnp.int32, (BLK, width), 1)
+        sublane = lax.broadcasted_iota(jnp.int32, (BLK, width), 0)
+        starts_at = range(0, width, BLK)
+
+        def column(row, first):
+            one = jnp.transpose(jnp.broadcast_to(row[:, first : first + BLK], (BLK, BLK)))
+            return jnp.concatenate([one] * (width // BLK), axis=1)
+
+        rank = jnp.zeros((1, width), jnp.int32)
+        for first in starts_at:
+            earlier = (column(given[2:3], first) == given[2:3]) & (sublane + first < lane)
+            rank += jnp.sum(jnp.where(earlier, 1, 0), axis=0, keepdims=True)
+        place = given[2:3] * DEPTH + rank
+        lefts = jnp.full((1, width), COLS * SLOTS, jnp.int32)
+        rights = jnp.zeros((1, width), jnp.int32)
+        for first in starts_at:
+            chosen = column(place, first) == lane
+            lefts += jnp.sum(jnp.where(chosen, column(given[0:1], first) - COLS * SLOTS, 0), axis=0, keepdims=True)
+            rights += jnp.sum(jnp.where(chosen, column(given[1:2], first), 0), axis=0, keepdims=True)
+        built[0:1] = lefts
+        built[1:2] = rights
+        done = pltpu.make_async_copy(built, table, n_r.at[5])
+        done.start()
+        done.wait()
 
     def gather(step):
         def level(m, number, waits):
@@ -196,7 +266,9 @@
         for m in range(CHUNKS):
             level(m, 1, (1, 2, 3))
             if m == 0:
+                pl.when(step == 0)(build_table)
                 prepare_own(step)
+                total(step, 0)
             prepare(m, (1, 2, 3))
             shared(m, 0)
             prepare_right(m, units_s[0])
@@ -243,7 +315,7 @@
             value = xs[block]
             keep_left(units_l[0], block, value)
             keep_right(units_r[0], block, value)
-            weight = table[SLOTS, block].astype(jnp.float32)
+            weight = table[2, block].astype(jnp.float32)
             terms[0] += folded(jnp.where(diagonal, value, 0.0)) * weight
             terms[1] += folded(value * value)
 
@@ -253,28 +325,40 @@
     def multiply(step, m):
         @pl.loop(m * CS, (m + 1) * CS)
         def _(target):
-            lhs = jnp.concatenate([ls[table[target, i]] for i in range(DEPTH)], axis=1)
-            rhs = jnp.concatenate([rs[table[target, DEPTH + i]] for i in range(DEPTH)], axis=0)
+            lhs = jnp.concatenate([ls[table[0, target * DEPTH + i]] for i in range(DEPTH)], axis=1)
+            rhs = jnp.concatenate([rs[table[1, target * DEPTH + i]] for i in range(DEPTH)], axis=0)
             found = jnp.dot(lhs, rhs, preferred_element_type=jnp.float32)
             squared = found[0:BLK, 0:BLK] + (
                 found[0:BLK, BLK : 2 * BLK] + found[BLK : 2 * BLK, 0:BLK] + found[BLK : 2 * BLK, BLK : 2 * BLK]
             )
             stored = xs[target]
-            xs[target] = coef[step, 0] * stored + coef[step, 1] * squared
-
-    for m in range(CHUNKS):
+            taken = (branches[step] == 1).astype(jnp.float32)
+            xs[target] = (2.0 - 2.0 * taken) * stored + (2.0 * taken - 1.0) * squared
+
+    def starts(m):
         remote = copy(x_hbm.at[part(m)], xs.at[part(m)], sw_s.at[m], sw_r.at[m], partner)
         local = pltpu.make_async_copy(x_hbm.at[part(m)], xs.at[part(m)], sw_r.at[m])
+        return remote, local
+
+    def beside(m):
+        return copy(x_hbm.at[part(m)], lf.at[units_l[3], part(m)], s_l.at[m, 2], r_l.at[m, 2], sibling)
+
+    for m in range(CHUNKS):
+        remote, local = starts(m)
+        pl.when(moved)(remote.start)
+        pl.when(moved)(beside(m).start)
+        pl.when(jnp.logical_not(moved))(local.start)
+    for remote, local in lists_copies():
         pl.when(moved)(remote.start)
         pl.when(jnp.logical_not(moved))(local.start)
     sums[...] = jnp.zeros_like(sums)
+    built[...] = jnp.zeros_like(built)
     ls[COLS * SLOTS] = jnp.zeros((2 * BLK, BLK), jnp.bfloat16)
     for m in range(CHUNKS):
-        remote = copy(x_hbm.at[part(m)], xs.at[part(m)], sw_s.at[m], sw_r.at[m], partner)
-        local = pltpu.make_async_copy(x_hbm.at[part(m)], xs.at[part(m)], sw_r.at[m])
+        remote, local = starts(m)
         pl.when(moved)(remote.wait)
         pl.when(jnp.logical_not(moved))(local.wait)
-        send_own(m)
+        send_own(m, first=True)
 
     def finals(m):
         remote = copy(xs.at[part(m)], out_hbm.at[part(m)], fin_s.at[m], fin_r.at[m], partner)
@@ -284,12 +368,13 @@
     @pl.loop(0, STEPS)
     def _(step):
         gather(step)
-        total(step, 0)
+        total(step, 1)
         for m in range(CHUNKS):
             multiply(step, m)
             if m == 0:
                 finish(step, CHUNKS - 1)
-            total(step, 1 + m)
+            if m % 2 == 1:
+                total(step, 2 + m // 2)
 
             @pl.when(step < STEPS - 1)
             def _():
@@ -302,24 +387,25 @@
                 pl.when(moved)(remote.start)
                 pl.when(jnp.logical_not(moved))(local.start)
 
-    total(STEPS - 1, CHUNKS + 1)
     for m in range(CHUNKS):
         remote, local = finals(m)
         pl.when(moved)(remote.wait)
         pl.when(jnp.logical_not(moved))(local.wait)
 
 
-def run(table, coef, blocks):
+def run(branches, rows, cols, lefts, rights, targets, blocks):
     dma = pltpu.SemaphoreType.DMA
     anywhere = pl.BlockSpec(memory_space=pl.ANY)
     scalars = pl.BlockSpec(memory_space=pltpu.SMEM)
+    width = SLOTS * DEPTH
+    count = targets.shape[1]
     return pl.pallas_call(
         kernel,
         out_shape=(
             jax.ShapeDtypeStruct((SLOTS, BLK, BLK), jnp.float32),
-            jax.ShapeDtypeStruct((STEPS, 2), jnp.float32),
+            jax.ShapeDtypeStruct((2, STEPS), jnp.float32),
         ),
-        in_specs=[scalars, scalars, anywhere],
+        in_specs=[scalars] + [anywhere] * 6,
         out_specs=(anywhere, scalars),
         scratch_shapes=[
             pltpu.VMEM((SLOTS, BLK, BLK), jnp.float32),
@@ -327,9 +413,17 @@
             pltpu.VMEM((ROWS, SLOTS, BLK, BLK), jnp.float32),
             pltpu.VMEM((COLS * SLOTS + 1, 2 * BLK, BLK), jnp.bfloat16),
             pltpu.VMEM((ROWS * SLOTS, BLK, 2 * BLK), jnp.bfloat16),
+            pltpu.VMEM((1, SLOTS), jnp.int32),
+            pltpu.VMEM((1, SLOTS), jnp.int32),
+            pltpu.VMEM((1, count), jnp.int32),
+            pltpu.VMEM((1, count), jnp.int32),
+            pltpu.VMEM((1, count), jnp.int32),
+            pltpu.VMEM((8, width), jnp.int32),
+            pltpu.VMEM((8, width), jnp.int32),
+            pltpu.SMEM((8, width), jnp.int32),
             pltpu.VMEM((2, 8, BLK), jnp.float32),
-            pltpu.VMEM((8, 8, BLK), jnp.float32),
-            pltpu.VMEM((7, 8, BLK), jnp.float32),
+            pltpu.VMEM((2, 8, BLK), jnp.float32),
+            pltpu.VMEM((3, 4, 8, BLK), jnp.float32),
             dma((CHUNKS, 7)),
             dma((CHUNKS, 15)),
             dma((CHUNKS, 7)),
@@ -338,53 +432,26 @@
             dma((CHUNKS,)),
             dma((CHUNKS,)),
             dma((CHUNKS,)),
-            dma((7,)),
-            dma((7,)),
+            dma((4, 3)),
+            dma((4, 3)),
+            dma((5,)),
+            dma((6,)),
             pltpu.SemaphoreType.REGULAR((CHUNKS,)),
         ],
         compiler_params=pltpu.CompilerParams(
-            collective_id=0, has_side_effects=True, vmem_limit_bytes=52 * 2**20
+            collective_id=0, has_side_effects=True, vmem_limit_bytes=VMEM_BYTES
         ),
         cost_estimate=pl.CostEstimate(
             flops=STEPS * SLOTS * DEPTH * 8 * BLK**3, bytes_accessed=2 * SLOTS * BLK * BLK * 4, transcendentals=0
         ),
-    )(table, coef, blocks)
-
-
-def product_table(left_ids, right_ids, target_ids):
-    count = target_ids.shape[0]
-    order = jnp.arange(count, dtype=jnp.int32)
-    same = (target_ids[:, None] == target_ids[None, :]) & (order[None, :] < order[:, None])
-    place = target_ids * DEPTH + jnp.sum(same.astype(jnp.int32), axis=1)
-    chosen = place[:, None] == jnp.arange(SLOTS * DEPTH, dtype=jnp.int32)[None, :]
-    lefts = jnp.sum(jnp.where(chosen, left_ids[:, None] - COLS * SLOTS, 0), axis=0) + COLS * SLOTS
-    rights = jnp.sum(jnp.where(chosen, right_ids[:, None], 0), axis=0)
-    return jnp.concatenate([lefts.reshape(SLOTS, DEPTH), rights.reshape(SLOTS, DEPTH)], axis=1)
-
-
-def partners():
-    pairs = []
-    for row in range(ROWS):
-        for col in range(COLS):
-            z, p = row % 4, col % 2
-            here = row * COLS + col
-            if p != zbits(z)[0]:
-                pairs.append((here, (row - z + z + 1 - 2 * (z % 2)) * COLS + col + 1 - 2 * p))
-            else:
-                pairs.append((here, here))
-    return pairs
+    )(branches, rows, cols, lefts, rights, targets, blocks)
 
 
 def body(x_tiles, block_rows, block_cols, pair_left, pair_right, pair_target, branches):
-    side_blocks = ROWS * BR
-    is_diagonal = (block_rows[0, 0] == block_cols[0, 0]) & (block_rows[0, 0] < side_blocks)
-    flags = jnp.pad(is_diagonal.astype(jnp.int32), (0, 2 * DEPTH - SLOTS))
-    table = jnp.concatenate([product_table(pair_left[0, 0], pair_right[0, 0], pair_target[0, 0]), flags[None]], axis=0)
-    table = lax.ppermute(table, ("row", "col"), partners())
-    taken = (branches == 1).astype(jnp.float32)
-    coef = jnp.stack([2.0 - 2.0 * taken, 2.0 * taken - 1.0], axis=1)
-    purified, traces = run(table, coef, x_tiles[0, 0])
-    return (purified[None, None], traces)
+    purified, traces = run(
+        branches, block_rows[0], block_cols[0], pair_left[0], pair_right[0], pair_target[0], x_tiles[0, 0]
+    )
+    return (purified[None, None], traces.T)
 
 
 def solution(mesh):

time: 232 us -> 209 us (0.901)
  Pallas kernels: 219 us -> 206 us
  starting transfers between devices: 4.93 us -> 0 us
    pallas_call x1, Pallas kernels: 219 us -> 206 us  [run(): pl.pallas_call(kernel, out_shape=(jax.ShapeDtypeStruct((SLOTS, BLK, BLK),...]
    ppermute x1 -> x0, starting transfers between devices: 4.93 us -> none  [body(): table = lax.ppermute(table, ('row', 'col'), partners())]
  transfers between devices with their start and end apart: 1 -> 0, of which waited for: 1 -> 0; matrix products, arithmetic and copies ran while one was open for 0% -> 0% of each run, Pallas kernels for 0% -> 0%
where the time goes in v4:
time: 209 us
  Pallas kernels  206 us (99%)
  local copies, waits for them, and re-layouts  2.63 us (1%)
    pallas_call x1, Pallas kernels, run(): pl.pallas_call(kernel, out_shape=(jax.ShapeDtypeStruct((SLOTS, BLK, BLK),...  206 us

profile of v4, /device:TPU:1, one launch (start us, length us, event | category | flops | bytes accessed | tf_op | source)
XLA Modules:
  0.0 209.1 jit_solution(11389500613705030723)
XLA Ops:
  0.6 205.8 %shard_map.86 = (f32[12,128,128]{2,1,0:T(8,128)}, f32[2,4]{1,0:T(2,128)}) custom-call(s32[4]{0:T(128)} %branches.1, s32[1,12]{1,0:T(1,128)} %bitcast.14, s32[1,12]{1,0:T(1,128)} %bitcast.15, s32[1,276]{1,0:T(1,128)} %bitcast.11, s32[1,276]{1,0:T(1,128)} %bitcast.12, s32[1,276]{1,0:T(1,128)} %bitcast.13, f32[12,128,128]{2,1,0:T(8,128)} %bitcast.10), custom_call_target="tpu_custom_call" | custom-call | flops 25769803776 | bytes 1572864 | tf_op jit(solution)/shard_map/pallas_call | solution.py:402
  206.5 0.0 copy-start
  206.5 2.1 copy.11
  208.5 0.0 copy-done
  208.6 0.6 copy.12
Async XLA Ops:
  206.5 2.1 copy-start

commit v5 on v4

--- a/solution.py
+++ b/solution.py
@@ -13,10 +13,13 @@
 ROWS = 16
 COLS = 8
 DEPTH = 32
-CHUNKS = 6
-CS = SLOTS // CHUNKS
+SIZES = (1, 2, 3, 3, 2, 1)
+CHUNKS = len(SIZES)
+STARTS = tuple(sum(SIZES[:m]) for m in range(CHUNKS))
 VMEM_BYTES = 60 * 2**20
-RELAYED = 2
+FORWARD = (2, 3)
+RELAYED = (1, 2)
+RELAYED_LAST = 5
 
 
 def zbits(z):
@@ -54,6 +57,29 @@
     )
     greeted = neighbours + (partner,) + tuple(devices[1] for _, devices in along)
 
+    def part(m):
+        return pl.ds(STARTS[m], SIZES[m])
+
+    def slots(m):
+        return pl.loop(STARTS[m], STARTS[m] + SIZES[m])
+
+    def copy(src, dst, ssem, rsem, device):
+        return pltpu.make_async_remote_copy(
+            src_ref=src, dst_ref=dst, send_sem=ssem, recv_sem=rsem, device_id=device, device_id_type=MESH
+        )
+
+    def starts(m):
+        return copy(x_hbm.at[part(m)], xs.at[part(m)], sw_s.at[m], sw_r.at[m], partner)
+
+    def starts_here(m):
+        return pltpu.make_async_copy(x_hbm.at[part(m)], xs.at[part(m)], sw_r.at[m])
+
+    for m in range(CHUNKS):
+        pl.when(jnp.logical_not(moved))(starts_here(m).start)
+    ls[COLS * SLOTS] = jnp.zeros((2 * BLK, BLK), jnp.bfloat16)
+    sums[...] = jnp.zeros_like(sums)
+    built[...] = jnp.zeros_like(built)
+
     barrier = pltpu.get_barrier_semaphore()
     for device in greeted:
         pl.semaphore_signal(barrier, inc=1, device_id=device, device_id_type=MESH)
@@ -68,16 +94,8 @@
     units_r = roles(x, high, lambda q, h: q * 4 + h * 3 + p * (1 - 2 * h))
     units_s = roles(x, high, lambda q, h: q * 4 + h * 3 + (1 - p) * (1 - 2 * h))
 
-    def part(m):
-        return pl.ds(m * CS, CS)
-
     def by_core(zero, one):
         return zero + p * (one - zero)
-
-    def copy(src, dst, ssem, rsem, device):
-        return pltpu.make_async_remote_copy(
-            src_ref=src, dst_ref=dst, send_sem=ssem, recv_sem=rsem, device_id=device, device_id_type=MESH
-        )
 
     class Gather:
         def __init__(self, buf, units, rsem, ssem, nxt, prv, pair):
@@ -86,24 +104,23 @@
 
         def plan(self, m):
             nxt, prv, pair = self.nxt, self.prv, self.pair
+            ahead = m in FORWARD
             first = [(0, nxt, 1), (0, prv, 2), (0, pair, 3)]
-            second = [(1, nxt, 4)] if m % 2 == 0 else [(2, prv, 4)]
-            relay = ([(1, pair, 5), (2, pair, 6)], [(4, pair, 7)])
-            onward = ([(3, nxt, 5), (3, prv, 6)], [(5, nxt, 7)] if m % 2 == 0 else [(6, prv, 7)])
+            opposite = (1, nxt, 4) if ahead else (2, prv, 4)
             unit = lambda sends: [(self.units[role], device, there) for role, device, there in sends]
-            ways = [[unit(way[level]) for way in (onward, relay)] for level in range(2)]
-            more = []
-            for level, (on, back) in enumerate(ways):
-                if m == RELAYED or (level == 1 and m == CHUNKS - 1):
-                    more.append(
-                        [
-                            (by_core(c, d), (by_core(e[0], f[0]), by_core(e[1], f[1])), there)
-                            for (c, e, there), (d, f, _) in zip(on, back)
-                        ]
-                    )
-                else:
-                    more.append(back if m < RELAYED else on)
-            return unit(first), unit(second) + more[0], more[1]
+            if m in RELAYED:
+                return [unit(sends) for sends in (first, [opposite, (1, pair, 5), (2, pair, 6)], [], [(4, pair, 7)])]
+            to_next, to_prev = (3, nxt, 5), (3, prv, 6)
+            on, end = (to_next, to_prev) if ahead else (to_prev, to_next)
+            last = (5, nxt, 7) if ahead else (6, prv, 7)
+            if m != RELAYED_LAST:
+                return [unit(sends) for sends in (first, [on], [opposite, end], [last])]
+            return [unit(sends) for sends in (first, [on, opposite], [end], [(4, pair, 7)])]
+
+        def sent_on(self, m):
+            if m in RELAYED:
+                return (4,)
+            return (4,) if m == RELAYED_LAST else ((5,) if m in FORWARD else (6,))
 
         def sends(self, m, level):
             plan = self.plan(m)
@@ -156,12 +173,12 @@
     def prepare_left(m, role):
         unit = units_l[role]
 
-        @pl.loop(m * CS, (m + 1) * CS)
+        @slots(m)
         def _(block):
             keep_left(unit, block, lf[unit, block])
 
     def prepare_right(m, unit):
-        @pl.loop(m * CS, (m + 1) * CS)
+        @slots(m)
         def _(block):
             keep_right(unit, block, rf[unit, block])
 
@@ -251,61 +268,93 @@
         done.wait()
 
     def gather(step):
-        def level(m, number, waits):
+        def arrive(m, waits):
             for role in waits:
                 left.arrived(m, role)
                 right.arrived(m, role)
-            for one in left.sends(m, number) + right.sends(m, number) + [share(m, role) for role in waits]:
+
+        def send(m, number):
+            for one in left.sends(m, number) + right.sends(m, number):
                 one.start()
+
+        def share_all(m, waits):
+            for role in waits:
+                share(m, role).start()
 
         def prepare(m, waits):
             for role in waits:
                 prepare_left(m, role)
                 prepare_right(m, units_r[role])
 
+        def prepare_shared(m, waits):
+            for role in waits:
+                shared(m, role)
+                prepare_right(m, units_s[role])
+
         for m in range(CHUNKS):
-            level(m, 1, (1, 2, 3))
+            arrive(m, (1, 2, 3))
+            send(m, 1)
+            if m == CHUNKS - 1:
+                for after in range(CHUNKS):
+                    send(after, 2)
+            share_all(m, (1, 2, 3))
             if m == 0:
                 pl.when(step == 0)(build_table)
                 prepare_own(step)
                 total(step, 0)
             prepare(m, (1, 2, 3))
-            shared(m, 0)
-            prepare_right(m, units_s[0])
+            prepare_shared(m, (0,))
         for m in range(CHUNKS):
-            level(m, 2, (4, 5, 6))
-            for role in (1, 2, 3):
-                shared(m, role)
-                prepare_right(m, units_s[role])
-            prepare(m, (4, 5, 6))
+            roles_now = left.sent_on(m)
+            arrive(m, roles_now)
+            send(m, 3)
+            share_all(m, roles_now)
+            prepare(m, roles_now)
+            prepare_shared(m, (1, 2, 3))
+        def take(m, waits):
+            for role in waits:
+                right.arrived(m, role)
+                share(m, role).start()
+            for role in waits:
+                left.arrived(m, role)
+            prepare(m, waits)
+
+        for m in range(CHUNKS):
+            take(m, [role for role in (4, 5, 6) if role not in left.sent_on(m)])
+        for m in range(CHUNKS):
+            right.arrived(m, 7)
+            share(m, 7).start()
+            prepare_right(m, units_r[7])
+            prepare_shared(m, (4, 5, 6))
+            if m > 0:
+                last_share(m - 1)
+            if m == CHUNKS - 2:
+                pl.when(step < STEPS - 1)(lambda: finish(0))
         for m in range(CHUNKS):
             left.arrived(m, 7)
-            right.arrived(m, 7)
-            share(m, 7).start()
-            prepare(m, (7,))
-            for role in (4, 5, 6):
-                shared(m, role)
-                prepare_right(m, units_s[role])
-            if m > 0:
-                last_share(m - 1)
-                finish(step, m - 1)
+            prepare_left(m, 7)
         last_share(CHUNKS - 1)
 
     def last_share(m):
         shared(m, 7)
         prepare_right(m, units_s[7])
 
-    def finish(step, m):
-        for number in range(3):
+    def sent_own(m):
+        for one in left.sends(m, 0) + right.sends(m, 0) + [share(m, 0)]:
+            one.wait_send()
+
+    def sent_rest(m):
+        for number in range(1, 4):
             for one in left.sends(m, number) + right.sends(m, number):
                 one.wait_send()
-        for role in range(8):
+        for role in range(1, 8):
             share(m, role).wait_send()
 
-        @pl.when(step < STEPS - 1)
-        def _():
-            for device in neighbours:
-                pl.semaphore_signal(credit.at[m], inc=1, device_id=device, device_id_type=MESH)
+    def finish(m):
+        sent_own(m)
+        sent_rest(m)
+        for device in neighbours:
+            pl.semaphore_signal(credit.at[m], inc=1, device_id=device, device_id_type=MESH)
 
     def prepare_own(step):
         terms[...] = jnp.zeros_like(terms)
@@ -323,7 +372,7 @@
             sums[0, pl.ds(2 * step + which, 1)] = jnp.sum(terms[which], axis=0, keepdims=True)
 
     def multiply(step, m):
-        @pl.loop(m * CS, (m + 1) * CS)
+        @slots(m)
         def _(target):
             lhs = jnp.concatenate([ls[table[0, target * DEPTH + i]] for i in range(DEPTH)], axis=1)
             rhs = jnp.concatenate([rs[table[1, target * DEPTH + i]] for i in range(DEPTH)], axis=0)
@@ -335,29 +384,18 @@
             taken = (branches[step] == 1).astype(jnp.float32)
             xs[target] = (2.0 - 2.0 * taken) * stored + (2.0 * taken - 1.0) * squared
 
-    def starts(m):
-        remote = copy(x_hbm.at[part(m)], xs.at[part(m)], sw_s.at[m], sw_r.at[m], partner)
-        local = pltpu.make_async_copy(x_hbm.at[part(m)], xs.at[part(m)], sw_r.at[m])
-        return remote, local
-
     def beside(m):
         return copy(x_hbm.at[part(m)], lf.at[units_l[3], part(m)], s_l.at[m, 2], r_l.at[m, 2], sibling)
 
     for m in range(CHUNKS):
-        remote, local = starts(m)
-        pl.when(moved)(remote.start)
+        pl.when(moved)(starts(m).start)
         pl.when(moved)(beside(m).start)
-        pl.when(jnp.logical_not(moved))(local.start)
     for remote, local in lists_copies():
         pl.when(moved)(remote.start)
         pl.when(jnp.logical_not(moved))(local.start)
-    sums[...] = jnp.zeros_like(sums)
-    built[...] = jnp.zeros_like(built)
-    ls[COLS * SLOTS] = jnp.zeros((2 * BLK, BLK), jnp.bfloat16)
     for m in range(CHUNKS):
-        remote, local = starts(m)
-        pl.when(moved)(remote.wait)
-        pl.when(jnp.logical_not(moved))(local.wait)
+        pl.when(moved)(starts(m).wait)
+        pl.when(jnp.logical_not(moved))(starts_here(m).wait)
         send_own(m, first=True)
 
     def finals(m):
@@ -370,16 +408,15 @@
         gather(step)
         total(step, 1)
         for m in range(CHUNKS):
+            pl.when(step == STEPS - 1)(lambda m=m: sent_own(m))
             multiply(step, m)
-            if m == 0:
-                finish(step, CHUNKS - 1)
-            if m % 2 == 1:
-                total(step, 2 + m // 2)
 
             @pl.when(step < STEPS - 1)
             def _():
                 pl.semaphore_wait(credit.at[m], len(neighbours))
                 send_own(m)
+                if m + 1 < CHUNKS:
+                    finish(m + 1)
 
             @pl.when(step == STEPS - 1)
             def _():
@@ -387,7 +424,11 @@
                 pl.when(moved)(remote.start)
                 pl.when(jnp.logical_not(moved))(local.start)
 
+            if m % 2 == 1:
+                total(step, 2 + m // 2)
+
     for m in range(CHUNKS):
+        sent_rest(m)
         remote, local = finals(m)
         pl.when(moved)(remote.wait)
         pl.when(jnp.logical_not(moved))(local.wait)
@@ -395,7 +436,7 @@
 
 def run(branches, rows, cols, lefts, rights, targets, blocks):
     dma = pltpu.SemaphoreType.DMA
-    anywhere = pl.BlockSpec(memory_space=pl.ANY)
+    main = pl.BlockSpec(memory_space=pltpu.HBM)
     scalars = pl.BlockSpec(memory_space=pltpu.SMEM)
     width = SLOTS * DEPTH
     count = targets.shape[1]
@@ -405,8 +446,8 @@
             jax.ShapeDtypeStruct((SLOTS, BLK, BLK), jnp.float32),
             jax.ShapeDtypeStruct((2, STEPS), jnp.float32),
         ),
-        in_specs=[scalars] + [anywhere] * 6,
-        out_specs=(anywhere, scalars),
+        in_specs=[scalars] + [main] * 6,
+        out_specs=(main, scalars),
         scratch_shapes=[
             pltpu.VMEM((SLOTS, BLK, BLK), jnp.float32),
             pltpu.VMEM((COLS, SLOTS, BLK, BLK), jnp.float32),

time: 209 us -> 208 us (level)
  no operation moved by 1% of the time
where the time goes in v5:
time: 208 us
  Pallas kernels  205 us (99%)
  local copies, waits for them, and re-layouts  2.63 us (1%)
    pallas_call x1, Pallas kernels, run(): pl.pallas_call(kernel, out_shape=(jax.ShapeDtypeStruct((SLOTS, BLK, BLK),...  205 us

profile of v5, /device:TPU:1, one launch (start us, length us, event | category | flops | bytes accessed | tf_op | source)
XLA Modules:
  0.0 208.0 jit_solution(3627654806147712750)
XLA Ops:
  0.6 204.8 %shard_map.86 = (f32[12,128,128]{2,1,0:T(8,128)}, f32[2,4]{1,0:T(2,128)}) custom-call(s32[4]{0:T(128)} %branches.1, s32[1,12]{1,0:T(1,128)} %bitcast.14, s32[1,12]{1,0:T(1,128)} %bitcast.15, s32[1,276]{1,0:T(1,128)} %bitcast.11, s32[1,276]{1,0:T(1,128)} %bitcast.12, s32[1,276]{1,0:T(1,128)} %bitcast.13, f32[12,128,128]{2,1,0:T(8,128)} %bitcast.10), custom_call_target="tpu_custom_call" | custom-call | flops 25769803776 | bytes 1572864 | tf_op jit(solution)/shard_map/pallas_call | solution.py:443
  205.4 0.0 copy-start
  205.4 2.1 copy.11
  207.5 0.0 copy-done
  207.5 0.6 copy.12
Async XLA Ops:
  205.4 2.1 copy-start

commit v6 on v5

--- a/solution.py
+++ b/solution.py
@@ -149,7 +149,7 @@
 
     def send_own(m, first=False):
         to_next, to_prev, to_pair = left.sends(m, 0)
-        for one in [to_next, to_prev] + right.sends(m, 0) + [share(m, 0)]:
+        for one in right.sends(m, 0) + [share(m, 0), to_next, to_prev]:
             one.start()
         if first:
             pl.when(jnp.logical_not(moved))(to_pair.start)
@@ -268,18 +268,19 @@
         done.wait()
 
     def gather(step):
-        def arrive(m, waits):
+        def send(side, m, number):
+            for one in side.sends(m, number):
+                one.start()
+
+        def pass_on(m, waits, number):
+            for role in waits:
+                right.arrived(m, role)
+            send(right, m, number)
+            for role in waits:
+                share(m, role).start()
             for role in waits:
                 left.arrived(m, role)
-                right.arrived(m, role)
-
-        def send(m, number):
-            for one in left.sends(m, number) + right.sends(m, number):
-                one.start()
-
-        def share_all(m, waits):
-            for role in waits:
-                share(m, role).start()
+            send(left, m, number)
 
         def prepare(m, waits):
             for role in waits:
@@ -292,12 +293,11 @@
                 prepare_right(m, units_s[role])
 
         for m in range(CHUNKS):
-            arrive(m, (1, 2, 3))
-            send(m, 1)
+            pass_on(m, (1, 2, 3), 1)
             if m == CHUNKS - 1:
                 for after in range(CHUNKS):
-                    send(after, 2)
-            share_all(m, (1, 2, 3))
+                    send(right, after, 2)
+                    send(left, after, 2)
             if m == 0:
                 pl.when(step == 0)(build_table)
                 prepare_own(step)
@@ -306,9 +306,7 @@
             prepare_shared(m, (0,))
         for m in range(CHUNKS):
             roles_now = left.sent_on(m)
-            arrive(m, roles_now)
-            send(m, 3)
-            share_all(m, roles_now)
+            pass_on(m, roles_now, 3)
             prepare(m, roles_now)
             prepare_shared(m, (1, 2, 3))
         def take(m, waits):

time: 208 us -> 208 us (level)
  no operation moved by 1% of the time
where the time goes in v6:
time: 208 us
  Pallas kernels  205 us (99%)
  local copies, waits for them, and re-layouts  2.63 us (1%)
    pallas_call x1, Pallas kernels, run(): pl.pallas_call(kernel, out_shape=(jax.ShapeDtypeStruct((SLOTS, BLK, BLK),...  205 us

profile of v6, /device:TPU:1, one launch (start us, length us, event | category | flops | bytes accessed | tf_op | source)
XLA Modules:
  0.0 208.0 jit_solution(15342013341127652509)
XLA Ops:
  0.6 204.7 %shard_map.86 = (f32[12,128,128]{2,1,0:T(8,128)}, f32[2,4]{1,0:T(2,128)}) custom-call(s32[4]{0:T(128)} %branches.1, s32[1,12]{1,0:T(1,128)} %bitcast.14, s32[1,12]{1,0:T(1,128)} %bitcast.15, s32[1,276]{1,0:T(1,128)} %bitcast.11, s32[1,276]{1,0:T(1,128)} %bitcast.12, s32[1,276]{1,0:T(1,128)} %bitcast.13, f32[12,128,128]{2,1,0:T(8,128)} %bitcast.10), custom_call_target="tpu_custom_call" | custom-call | flops 25769803776 | bytes 1572864 | tf_op jit(solution)/shard_map/pallas_call | solution.py:441
  205.4 0.0 copy-start
  205.4 2.1 copy.11
  207.4 0.0 copy-done
  207.4 0.6 copy.12
Async XLA Ops:
  205.4 2.1 copy-start
